TPU v7x, 32 devices: a whole 2x2x4 slice. The times are simulated.
32 devices in a mesh: row: 16 (over z, y, x), col: 2 (over core).
Axes of the slice: x: 2, y: 2, z: 4, core: 2. Of those that a mesh axis runs over, the one named last changes fastest.
Arguments:
- panel: float32 [8192, 2048], P('row', 'col'), may hold values from -6 to 6
- inner_vecs: float32 [16, 4, 256, 128], P('row', None, 'col'), may hold values from -0.375 to 0.375
- inner_factor: float32 [16, 4, 128, 128], P('row'), may hold values from -0.5 to 0.5
- border_vecs: float32 [16, 4, 256, 128], P('row', None, 'col'), may hold values from -0.375 to 0.375
- border_factor: float32 [16, 4, 128, 128], P('row'), may hold values from -0.5 to 0.5
- group_start: int32 [4], replicated, may hold values from 0 to 12
- group_span: int32 [4], replicated, may hold values from 3 to 15
Outputs:
- panel_out: float32 [8192, 2048], P('row', 'col')
All inputs are finite; a program needn't handle non-finite values.
Results may differ from a plain program's by a relative error of at most 0.00011.
Values sent between devices are 32-bit elements; how exact they have to be, the bound alone decides.
No kernel may reach another device: no remote copies, remote signals or barrier semaphores. Data moves between devices by JAX's collectives and lax.ppermute only.
A program may use at most 64 MiB of HBM per device.

v0:
```python
import jax
import jax.numpy as jnp
from jax import lax
from jax.sharding import PartitionSpec as P


def from_behind(value, axis, by):
    devices = lax.axis_size(axis)
    pairs = [(i, i + by) for i in range(devices) if 0 <= i + by < devices]
    return lax.ppermute(value, axis, pairs)


def project(vectors, band):
    return jnp.einsum("bk,bc->kc", vectors, band, precision=lax.Precision.HIGHEST)


def expand(vectors, factor, inner):
    scaled = jnp.dot(factor, inner, precision=lax.Precision.HIGHEST)
    return jnp.dot(vectors, scaled, precision=lax.Precision.HIGHEST)


def reflect(vectors, factor, band):
    return expand(vectors, factor, project(vectors, band))


def local(panel, inner_vecs, inner_factor, border_vecs, border_factor, group_start, group_span):
    width = inner_factor.shape[-1]
    height = panel.shape[0]
    steps = inner_factor.shape[1]
    index = lax.axis_index("row")
    whole_inner, whole_border = (
        lax.all_gather(inner_vecs, "col", axis=2, tiled=True),
        lax.all_gather(border_vecs, "col", axis=2, tiled=True),
    )
    whole_inner = whole_inner[0]
    whole_border = whole_border[0]
    fac_inner = inner_factor[0]
    fac_border = border_factor[0]
    lower_vecs, lower_factor = from_behind(
        (whole_border[0::2, width:, :], fac_border[0::2]), "row", 1
    )
    for step in range(steps):
        start = group_start[step]
        span = group_span[step]
        active = (index >= start) & (index < start + span)
        if step % 2 == 1:
            upper = panel[: 2 * width]
            panel = panel.at[: 2 * width].set(
                upper - reflect(whole_inner[step], fac_inner[step], upper)
            )
            lower = panel[2 * width :]
            change = reflect(whole_border[step], fac_border[step], lower)
            change = jnp.where(active, change, jnp.zeros_like(change))
            panel = panel.at[2 * width :].set(lower - change)
            continue
        middle = panel[width : 3 * width]
        panel = panel.at[width : 3 * width].set(
            middle - reflect(whole_inner[step], fac_inner[step], middle)
        )
        half_step = step // 2
        upper_vecs = whole_border[step][:width]
        upper_part = project(upper_vecs, panel[height - width :])
        lower_part = project(lower_vecs[half_step], panel[:width])
        from_below = from_behind(lower_part, "row", -1)
        from_above = from_behind(upper_part, "row", 1)
        previous = (index - 1 >= start) & (index - 1 < start + span)
        own_change = expand(upper_vecs, fac_border[step], upper_part + from_below)
        own_change = jnp.where(active, own_change, jnp.zeros_like(own_change))
        prior_change = expand(
            lower_vecs[half_step], lower_factor[half_step], from_above + lower_part
        )
        prior_change = jnp.where(previous, prior_change, jnp.zeros_like(prior_change))
        panel = panel.at[height - width :].set(panel[height - width :] - own_change)
        panel = panel.at[:width].set(panel[:width] - prior_change)
    return panel


def solution(mesh):
    placed = (
        P("row", "col"),
        P("row", None, "col", None),
        P("row", None, None, None),
        P("row", None, "col", None),
        P("row", None, None, None),
        P(),
        P(),
    )
    return jax.shard_map(
        local, mesh=mesh, in_specs=placed, out_specs=P("row", "col"), check_vma=False
    )
```

profile of v0, /device:TPU:0, one launch (start us, length us, event | category | flops | bytes accessed | tf_op | source)
XLA Modules:
  0.0 102.8 jit_solution(427138683400231934)
XLA Ops:
  0.0 2.5 %all_gather.7 = f32[1,4,256,128]{3,2,1,0:T(8,128)S(1)} all-gather(f32[1,4,128,128]{3,2,1,0:T(8,128)} %param.30), channel_id=1, replica_groups=mesh['row'=16,'col'=2] {'col'}, dimensions={2}, use_global_device_ids=true | all-gather | bytes 786432 | tf_op jit(solution)/shard_map/all_gather | solution.py:33
  2.5 0.7 slice.335
  3.1 4.8 %collective-permute-start = (f32[2,128,128]{2,1,0:T(8,128)}, f32[2,128,128]{2,1,0:T(8,128)S(1)}, u32[]{:S(2)}, u32[]{:S(2)}) collective-permute-start(f32[2,128,128]{2,1,0:T(8,128)} %slice.335), channel_id=1, source_target_pairs={{0,2},{2,4},{4,6},{6,8},{8,10},{10,12},{12,14},{14,16},{16,18},{18... | collective-permute-start | bytes 393224 | tf_op jit(solution)/shard_map/ppermute | solution.py:10
  7.9 2.4 %all_gather.6 = f32[1,4,256,128]{3,2,1,0:T(8,128)S(1)} all-gather(f32[1,4,128,128]{3,2,1,0:T(8,128)} %param.28), channel_id=1, replica_groups=mesh['row'=16,'col'=2] {'col'}, dimensions={2}, use_global_device_ids=true | all-gather | bytes 786432 | tf_op jit(solution)/shard_map/all_gather | solution.py:32
  10.3 1.9 %copy.9 = f32[512,1024]{0,1:T(8,128)S(1)} copy(f32[512,1024]{1,0:T(8,128)} %param.27) | data formatting | bytes 4194304 | tf_op args[0]
  12.2 1.3 %fusion.36 = f32[128,1024]{1,0:T(8,128)S(1)} fusion(f32[512,1024]{0,1:T(8,128)S(1)} %copy.9, f32[1,4,256,128]{3,2,1,0:T(8,128)S(1)} %all_gather.6), kind=kOutput, calls=%fused_computation.50 | convolution fusion | flops 402653184 | bytes 1703936 | tf_op jit(solution)/shard_map/bk,bc->kc/dot_general | solution.py:14
  13.5 1.8 %fusion.62 = f32[1024,128]{1,0:T(8,128)S(1)} fusion(f32[128,1024]{1,0:T(8,128)S(1)} %fusion.36, f32[1,4,128,128]{3,2,1,0:T(8,128)} %param.29), kind=kOutput, calls=%fused_computation.88 | convolution fusion | flops 201326592 | bytes 1114112 | tf_op jit(solution)/shard_map/dot_general | solution.py:18
  15.3 0.0 copy-start
  15.3 0.0 copy-start.2
  15.3 0.0 copy-start.3
  15.3 1.4 %fusion.13 = f32[512,1024]{0,1:T(8,128)S(1)} fusion(f32[512,1024]{0,1:T(8,128)S(1)} %copy.9, f32[1024,128]{1,0:T(8,128)S(1)} %fusion.62, f32[1,4,256,128]{3,2,1,0:T(8,128)S(1)} %all_gather.6), kind=kOutput, calls=%fused_computation.19 | convolution fusion | flops 402915328 | bytes 2752512 | tf_op jit(solution)/shard_map/dot_general | solution.py:19
  16.8 1.4 %convolution_bitcast_fusion.7 = f32[128,1024]{0,1:T(8,128)} fusion(f32[512,1024]{0,1:T(8,128)S(1)} %fusion.13, f32[1,4,256,128]{3,2,1,0:T(8,128)S(1)} %all_gather.7), kind=kOutput, calls=%fused_computation.39 | convolution fusion | flops 201326592 | bytes 1114112 | tf_op jit(solution)/shard_map/bk,bc->kc/dot_general | solution.py:14
  18.1 4.2 %collective-permute-start.2 = (f32[128,1024]{0,1:T(8,128)}, f32[128,1024]{0,1:T(8,128)}, u32[]{:S(2)}, u32[]{:S(2)}) collective-permute-start(f32[128,1024]{0,1:T(8,128)} %convolution_bitcast_fusion.7), channel_id=1, source_target_pairs={{0,2},{2,4},{4,6},{6,8},{8,10},{10,12},{12,14},{14,16},{16,18},{18... | collective-permute-start | bytes 1572872 | tf_op jit(solution)/shard_map/ppermute | solution.py:10
  22.3 0.0 collective-permute-done
  22.3 1.3 %convolution_bitcast_fusion.6 = f32[128,1024]{0,1:T(8,128)} fusion(f32[512,1024]{0,1:T(8,128)S(1)} %fusion.13, f32[2,128,128]{2,1,0:T(8,128)S(1)} %collective-permute-done), kind=kOutput, calls=%fused_computation.38 | convolution fusion | flops 201326592 | bytes 1114112 | tf_op jit(solution)/shard_map/bk,bc->kc/dot_general | solution.py:14
  23.7 1.3 %collective-permute-start.1 = (f32[128,1024]{0,1:T(8,128)}, f32[128,1024]{0,1:T(8,128)}, u32[]{:S(2)}, u32[]{:S(2)}) collective-permute-start(f32[128,1024]{0,1:T(8,128)} %convolution_bitcast_fusion.6), channel_id=1, source_target_pairs={{2,0},{4,2},{6,4},{8,6},{10,8},{12,10},{14,12},{16,14},{18,16},{20... | collective-permute-start | bytes 1572872 | tf_op jit(solution)/shard_map/ppermute | solution.py:10
  24.9 0.0 copy-done
  24.9 0.7 slice.339
  25.6 5.2 %collective-permute-start.3 = (f32[2,128,128]{2,1,0:T(8,128)}, f32[2,128,128]{2,1,0:T(8,128)}, u32[]{:S(2)}, u32[]{:S(2)}) collective-permute-start(f32[2,128,128]{2,1,0:T(8,128)} %slice.339), channel_id=1, source_target_pairs={{0,2},{2,4},{4,6},{6,8},{8,10},{10,12},{12,14},{14,16},{16,18},{18... | collective-permute-start | bytes 393224 | tf_op jit(solution)/shard_map/ppermute | solution.py:10
  30.8 0.0 copy-done.2
  30.8 0.7 fusion.73
  32.7 0.0 copy-done.3
  32.7 0.7 fusion.72
  36.4 10.9 %collective-permute-done.3 = f32[2,128,128]{2,1,0:T(8,128)} collective-permute-done((f32[2,128,128]{2,1,0:T(8,128)}, f32[2,128,128]{2,1,0:T(8,128)}, u32[]{:S(2)}, u32[]{:S(2)}) %collective-permute-start.3) | collective-permute-done | bytes 131104 | tf_op jit(solution)/shard_map/ppermute | solution.py:10
  47.3 0.0 collective-permute-done.2
  47.3 1.8 %fusion.44 = f32[1024,128]{1,0:T(8,128)S(1)} fusion(f32[128,1024]{0,1:T(8,128)} %collective-permute-done.2, f32[128,1024]{0,1:T(8,128)} %convolution_bitcast_fusion.6, f32[2,128,128]{2,1,0:T(8,128)} %collective-permute-done.3), kind=kOutput, calls=%fused_computation.58 | convolution fusion | flops 201457664 | bytes 1638400 | tf_op jit(solution)/shard_map/dot_general | solution.py:18
  49.1 0.0 collective-permute-done.1
  49.1 1.8 %fusion.46 = f32[1024,128]{1,0:T(8,128)S(1)} fusion(f32[128,1024]{0,1:T(8,128)} %convolution_bitcast_fusion.7, f32[128,1024]{0,1:T(8,128)} %collective-permute-done.1, f32[1,4,128,128]{3,2,1,0:T(8,128)S(1)} %copy-done), kind=kOutput, calls=%fused_computation.60 | convolution fusion | flops 201457664 | bytes 1638400 | tf_op jit(solution)/shard_map/dot_general | solution.py:18
  50.9 0.0 copy-start.1
  50.9 0.8 fusion.25
  51.8 0.8 fusion.22
  52.6 1.0 fusion.34
  53.6 0.0 copy-done.1
  53.6 0.6 fusion.59
  54.2 1.4 %fusion.11 = f32[512,1024]{0,1:T(8,128)S(1)} fusion(f32[512,1024]{0,1:T(8,128)S(1)} %fusion.22, f32[1024,128]{1,0:T(8,128)S(1)} %fusion.59, f32[1,4,256,128]{3,2,1,0:T(8,128)S(1)} %all_gather.6), kind=kOutput, calls=%fused_computation.16 | convolution fusion | flops 402915328 | bytes 2752512 | tf_op jit(solution)/shard_map/dot_general | solution.py:19
  55.6 1.0 fusion.32
  56.6 0.6 fusion.57
  57.2 1.5 %fusion.2 = f32[512,1024]{0,1:T(8,128)S(1)} fusion(f32[512,1024]{0,1:T(8,128)S(1)} %fusion.11, f32[1024,128]{1,0:T(8,128)S(1)} %fusion.57, pred[]{:T(512)S(6)} %and.51, f32[1,4,256,128]{3,2,1,0:T(8,128)S(1)} %all_gather.7), kind=kOutput, calls=%fused_computation.4 | convolution fusion | flops 403177472 | bytes 2752513 | tf_op jit(solution)/shard_map/dot_general | solution.py:19
  58.7 1.0 fusion.30
  59.7 0.6 fusion.55
  60.3 1.4 %fusion.9 = f32[512,1024]{0,1:T(8,128)S(1)} fusion(f32[512,1024]{0,1:T(8,128)S(1)} %fusion.2, f32[1024,128]{1,0:T(8,128)S(1)} %fusion.55, f32[1,4,256,128]{3,2,1,0:T(8,128)S(1)} %all_gather.6), kind=kOutput, calls=%fused_computation.13 | convolution fusion | flops 402915328 | bytes 2752512 | tf_op jit(solution)/shard_map/dot_general | solution.py:19
  61.7 1.6 %convolution_bitcast_fusion.4 = f32[128,1024]{0,1:T(8,128)} fusion(f32[512,1024]{0,1:T(8,128)S(1)} %fusion.9, f32[2,128,128]{2,1,0:T(8,128)S(1)} %collective-permute-done), kind=kOutput, calls=%fused_computation.28 | convolution fusion | flops 201326592 | bytes 1114112 | tf_op jit(solution)/shard_map/bk,bc->kc/dot_general | solution.py:14
  63.3 1.3 %collective-permute-start.4 = (f32[128,1024]{0,1:T(8,128)}, f32[128,1024]{0,1:T(8,128)}, u32[]{:S(2)}, u32[]{:S(2)}) collective-permute-start(f32[128,1024]{0,1:T(8,128)} %convolution_bitcast_fusion.4), channel_id=1, source_target_pairs={{2,0},{4,2},{6,4},{8,6},{10,8},{12,10},{14,12},{16,14},{18,16},{20... | collective-permute-start | bytes 1572872 | tf_op jit(solution)/shard_map/ppermute | solution.py:10
  68.8 0.6 convolution_bitcast_fusion.5
  69.3 5.0 %collective-permute-start.5 = (f32[128,1024]{0,1:T(8,128)S(1)}, f32[128,1024]{0,1:T(8,128)S(1)}, u32[]{:S(2)}, u32[]{:S(2)}) collective-permute-start(f32[128,1024]{0,1:T(8,128)S(1)} %convolution_bitcast_fusion.5), channel_id=1, source_target_pairs={{0,2},{2,4},{4,6},{6,8},{8,10},{10,12},{12,14},{14,16},{16,18},{18... | collective-permute-start | bytes 1572872 | tf_op jit(solution)/shard_map/ppermute | solution.py:10
  74.4 6.4 %collective-permute-done.4 = f32[128,1024]{0,1:T(8,128)} collective-permute-done((f32[128,1024]{0,1:T(8,128)}, f32[128,1024]{0,1:T(8,128)}, u32[]{:S(2)}, u32[]{:S(2)}) %collective-permute-start.4) | collective-permute-done | bytes 524320 | tf_op jit(solution)/shard_map/ppermute | solution.py:10
  80.8 1.6 %fusion.42 = f32[1024,128]{1,0:T(8,128)S(1)} fusion(f32[128,1024]{0,1:T(8,128)S(1)} %convolution_bitcast_fusion.5, f32[128,1024]{0,1:T(8,128)} %collective-permute-done.4, f32[1,4,128,128]{3,2,1,0:T(8,128)S(1)} %copy-done), kind=kOutput, calls=%fused_computation.56 | convolution fusion | flops 201457664 | bytes 1638400 | tf_op jit(solution)/shard_map/dot_general | solution.py:18
  82.4 0.8 fusion.19
  83.2 8.4 %collective-permute-done.5 = f32[128,1024]{0,1:T(8,128)S(1)} collective-permute-done((f32[128,1024]{0,1:T(8,128)S(1)}, f32[128,1024]{0,1:T(8,128)S(1)}, u32[]{:S(2)}, u32[]{:S(2)}) %collective-permute-start.5) | collective-permute-done | bytes 524320 | tf_op jit(solution)/shard_map/ppermute | solution.py:10
  91.6 1.6 %fusion.40 = f32[1024,128]{1,0:T(8,128)S(1)} fusion(f32[128,1024]{0,1:T(8,128)S(1)} %collective-permute-done.5, f32[128,1024]{0,1:T(8,128)} %convolution_bitcast_fusion.4, f32[2,128,128]{2,1,0:T(8,128)} %collective-permute-done.3), kind=kOutput, calls=%fused_computation.54 | convolution fusion | flops 201457664 | bytes 1638400 | tf_op jit(solution)/shard_map/dot_general | solution.py:18
  93.2 0.8 fusion.16
  94.0 1.0 fusion.28
  95.0 1.4 %fusion.52 = f32[1024,128]{1,0:T(8,128)S(1)} fusion(f32[1024,128]{1,0:T(8,128)S(1)} %fusion.28, f32[1,4,128,128]{3,2,1,0:T(8,128)} %param.29), kind=kOutput, calls=%fused_computation.78 | convolution fusion | flops 201326592 | bytes 1114112 | tf_op jit(solution)/shard_map/dot_general | solution.py:18
  96.5 1.4 %fusion.7 = f32[512,1024]{0,1:T(8,128)S(1)} fusion(f32[512,1024]{0,1:T(8,128)S(1)} %fusion.16, f32[1024,128]{1,0:T(8,128)S(1)} %fusion.52, f32[1,4,256,128]{3,2,1,0:T(8,128)S(1)} %all_gather.6), kind=kOutput, calls=%fused_computation.10 | convolution fusion | flops 402915328 | bytes 2752512 | tf_op jit(solution)/shard_map/dot_general | solution.py:19
  97.9 1.0 fusion.26
  98.9 0.6 fusion.50
  99.5 1.5 %fusion.5 = f32[512,1024]{0,1:T(8,128)S(1)} fusion(f32[512,1024]{0,1:T(8,128)S(1)} %fusion.7, f32[1024,128]{1,0:T(8,128)S(1)} %fusion.50, pred[]{:T(512)S(6)} %and.54, f32[1,4,256,128]{3,2,1,0:T(8,128)S(1)} %all_gather.7), kind=kOutput, calls=%fused_computation.7 | convolution fusion | flops 403177472 | bytes 2752513 | tf_op jit(solution)/shard_map/dot_general | solution.py:19
  100.9 1.8 %copy.10 = f32[512,1024]{1,0:T(8,128)} copy(f32[512,1024]{0,1:T(8,128)S(1)} %fusion.5) | data formatting | bytes 4194304 | tf_op jit(solution)/shard_map/scatter | solution.py:54
Async XLA Ops:
  3.1 19.2 %collective-permute-start = (f32[2,128,128]{2,1,0:T(8,128)}, f32[2,128,128]{2,1,0:T(8,128)S(1)}, u32[]{:S(2)}, u32[]{:S(2)}) collective-permute-start(f32[2,128,128]{2,1,0:T(8,128)} %slice.335), channel_id=1, source_target_pairs={{0,2},{2,4},{4,6},{6,8},{8,10},{10,12},{12,14},{14,16},{16,18},{18... | collective-permute-start | bytes 393224 | tf_op jit(solution)/shard_map/ppermute | solution.py:10
  15.3 9.6 %copy-start = (f32[1,4,128,128]{3,2,1,0:T(8,128)S(1)}, f32[1,4,128,128]{3,2,1,0:T(8,128)}, u32[]{:S(2)}) copy-start(f32[1,4,128,128]{3,2,1,0:T(8,128)} %param.31) | copy-start | bytes 786436
  15.3 15.5 %copy-start.2 = (s32[4]{0:T(128)S(1)}, s32[4]{0:T(128)}, u32[]{:S(2)}) copy-start(s32[4]{0:T(128)} %param.32) | copy-start | bytes 52
  15.3 17.4 %copy-start.3 = (s32[4]{0:T(128)S(1)}, s32[4]{0:T(128)}, u32[]{:S(2)}) copy-start(s32[4]{0:T(128)} %param.33) | copy-start | bytes 52
  18.1 29.2 %collective-permute-start.2 = (f32[128,1024]{0,1:T(8,128)}, f32[128,1024]{0,1:T(8,128)}, u32[]{:S(2)}, u32[]{:S(2)}) collective-permute-start(f32[128,1024]{0,1:T(8,128)} %convolution_bitcast_fusion.7), channel_id=1, source_target_pairs={{0,2},{2,4},{4,6},{6,8},{8,10},{10,12},{12,14},{14,16},{16,18},{18... | collective-permute-start | bytes 1572872 | tf_op jit(solution)/shard_map/ppermute | solution.py:10
  23.7 25.5 %collective-permute-start.1 = (f32[128,1024]{0,1:T(8,128)}, f32[128,1024]{0,1:T(8,128)}, u32[]{:S(2)}, u32[]{:S(2)}) collective-permute-start(f32[128,1024]{0,1:T(8,128)} %convolution_bitcast_fusion.6), channel_id=1, source_target_pairs={{2,0},{4,2},{6,4},{8,6},{10,8},{12,10},{14,12},{16,14},{18,16},{20... | collective-permute-start | bytes 1572872 | tf_op jit(solution)/shard_map/ppermute | solution.py:10
  25.6 21.7 %collective-permute-start.3 = (f32[2,128,128]{2,1,0:T(8,128)}, f32[2,128,128]{2,1,0:T(8,128)}, u32[]{:S(2)}, u32[]{:S(2)}) collective-permute-start(f32[2,128,128]{2,1,0:T(8,128)} %slice.339), channel_id=1, source_target_pairs={{0,2},{2,4},{4,6},{6,8},{8,10},{10,12},{12,14},{14,16},{16,18},{18... | collective-permute-start | bytes 393224 | tf_op jit(solution)/shard_map/ppermute | solution.py:10
  50.9 2.7 %copy-start.1 = (f32[1,4,128,128]{3,2,1,0:T(8,128)S(1)}, f32[1,4,128,128]{3,2,1,0:T(8,128)}, u32[]{:S(2)}) copy-start(f32[1,4,128,128]{3,2,1,0:T(8,128)} %param.29) | copy-start | bytes 786436
  63.3 17.5 %collective-permute-start.4 = (f32[128,1024]{0,1:T(8,128)}, f32[128,1024]{0,1:T(8,128)}, u32[]{:S(2)}, u32[]{:S(2)}) collective-permute-start(f32[128,1024]{0,1:T(8,128)} %convolution_bitcast_fusion.4), channel_id=1, source_target_pairs={{2,0},{4,2},{6,4},{8,6},{10,8},{12,10},{14,12},{16,14},{18,16},{20... | collective-permute-start | bytes 1572872 | tf_op jit(solution)/shard_map/ppermute | solution.py:10
  69.3 22.2 %collective-permute-start.5 = (f32[128,1024]{0,1:T(8,128)S(1)}, f32[128,1024]{0,1:T(8,128)S(1)}, u32[]{:S(2)}, u32[]{:S(2)}) collective-permute-start(f32[128,1024]{0,1:T(8,128)S(1)} %convolution_bitcast_fusion.5), channel_id=1, source_target_pairs={{0,2},{2,4},{4,6},{6,8},{8,10},{10,12},{12,14},{14,16},{16,18},{18... | collective-permute-start | bytes 1572872 | tf_op jit(solution)/shard_map/ppermute | solution.py:10
where the time goes:
time: 105 us; the launch traced here: 103 us
  matrix products  35.3 us (34%)
  waiting for transfers between devices  25.7 us (24%)
  starting transfers between devices  21.7 us (21%)
  between operations  8.8 us (8%)
  local copies, waits for them, and re-layouts  6.4 us (6%)
  blocking collectives  4.85 us (5%)
    ppermute x6, waiting for transfers between devices, from_behind(): return lax.ppermute(value, axis, pairs)  25.7 us
    ppermute x6, starting transfers between devices, from_behind(): return lax.ppermute(value, axis, pairs)  21.7 us
    dot_general x10, matrix products, expand(): scaled = jnp.dot(factor, inner, precision=lax.Precision.HIGHEST)  12.4 us
    dot_general x10, matrix products, expand(): return jnp.dot(vectors, scaled, precision=lax.Precision.HIGHEST)  11.8 us
    dot_general x10, matrix products, project(): jnp.einsum('bk,bc->kc', vectors, band, precision=lax.Precision.HIGHEST)  11.1 us
    all_gather x1, blocking collectives, local(): lax.all_gather(border_vecs, 'col', axis=2, tiled=True)  2.46 us
    all_gather x1, blocking collectives, local(): lax.all_gather(inner_vecs, 'col', axis=2, tiled=True)  2.39 us
  transfers between devices with their start and end apart: 6, of which 3 were waited for; matrix products, arithmetic and copies ran while one was open for 15% of the time, Pallas kernels for 0%

commit v1 on v0

v1 whole, which is shorter than its diff:
```python
import jax
import jax.numpy as jnp
from jax import lax
from jax.experimental import pallas as pl
from jax.experimental.pallas import tpu as pltpu
from jax.sharding import PartitionSpec as P

F32 = jnp.float32
TILES = 4
VMEM_LIMIT = 24 * 1024 * 1024


def from_behind(value, axis, by):
    devices = lax.axis_size(axis)
    pairs = [(i, i + by) for i in range(devices) if 0 <= i + by < devices]
    return lax.ppermute(value, axis, pairs)


def other_core(value):
    cores = lax.axis_size("col")
    return lax.ppermute(value, "col", [(i, (i + 1) % cores) for i in range(cores)])


def exact_dot(x, y, contract=(1, 0)):
    return lax.dot_general(
        x,
        y,
        (((contract[0],), (contract[1],)), ((), ())),
        precision=lax.Precision.HIGHEST,
        preferred_element_type=F32,
    )


def split(x):
    high = x.astype(jnp.bfloat16)
    return high, (x - high.astype(F32)).astype(jnp.bfloat16)


def dot(x, y):
    xh, xl = split(x)
    yh, yl = split(y)
    small = jnp.dot(xl, yh, preferred_element_type=F32) + jnp.dot(
        xh, yl, preferred_element_type=F32
    )
    return small + jnp.dot(xh, yh, preferred_element_type=F32)


def change_of(first, second, factor, core):
    upper = jnp.where(core == 0, first, second)
    lower = jnp.where(core == 0, second, first)
    vectors = jnp.concatenate([upper, lower], axis=0)
    return exact_dot(exact_dot(vectors, factor), vectors, (1, 1))


def stacked(upper, lower):
    return jnp.concatenate([upper, lower], axis=0)


def is_active(flags, step):
    return flags[step] != 0


def first_kernel(flags, own, other, factor, b, c, early, bc, message):
    tile = pl.program_id(0)
    width = factor.shape[-1]

    @pl.when(tile == 0)
    def _():
        core = flags[5]
        for step in range(2):
            early[step] = change_of(own[step], other[step], factor[step], core)

    band = stacked(b[...], c[...])
    band = band - dot(early[0], band)
    bc[...] = band
    message[:width] = dot(early[1, :width, width:], band[:width])
    span = message.shape[1]
    for block in range(span // width):
        message[width:, block * width : (block + 1) * width] = early[
            1, pl.ds((tile * (span // width) + block) * (message.shape[0] - width), message.shape[0] - width), :width
        ]


def matrix_kernel(flags, own_i, other_i, fac_i, own_b, other_b, fac_b, late, border):
    core = flags[5]
    for step in range(late.shape[0]):
        late[step] = change_of(own_i[step + 2], other_i[step + 2], fac_i[step + 2], core)
    for step in range(border.shape[0]):
        border[step] = change_of(own_b[step], other_b[step], fac_b[step], core)


def second_kernel(flags, d, below, c, border, message, cd):
    width = d.shape[0]
    band = stacked(d[...], below[...])
    band = jnp.where(is_active(flags, 0), band - dot(border[0], band), band)
    message[...] = band[width:]
    band = stacked(c[...], band[:width])
    cd[...] = jnp.where(is_active(flags, 1), band - dot(border[1], band), band)


def third_kernel(flags, below, message, mixing, d, border, sent, d_out):
    width = d.shape[0]
    span = message.shape[1]
    low = below[...]
    low = low - dot(mixing[...], low) - message[...]
    band = stacked(d[...], low)
    band = jnp.where(is_active(flags, 2), band - dot(border[0], band), band)
    d_out[...] = band[:width]
    sent[...] = band[width:]


def fourth_kernel(flags, raw, above, b, c, d, second, late, border, out):
    width = raw.shape[0]
    first = flags[4] != 0
    ab = stacked(jnp.where(first, raw[...], above[...]), b[...])
    ab = ab - dot(second[0], ab)
    bc = stacked(ab[width:], c[...])
    bc = bc - dot(late[0], bc)
    cd = stacked(bc[width:], d[...])
    out[2 * width :] = jnp.where(is_active(flags, 3), cd - dot(border[0], cd), cd)
    ab = stacked(jnp.where(first, ab[:width], 0.0), bc[:width])
    out[: 2 * width] = ab - dot(late[1], ab)


def last_kernel(above, late, before, out):
    width = above.shape[0]
    top = above[...]
    change = dot(late[0], top)
    out[:width] = before[:width] + (top - change[:width])
    out[width:] = before[width:] - change[width:]


def smem():
    return pl.BlockSpec(memory_space=pltpu.SMEM)


def whole(shape, index=None):
    index = (0,) * len(shape) if index is None else index
    return pl.BlockSpec(shape, lambda tile: index)


def columns(rows, span, row=0):
    return pl.BlockSpec((rows, span), lambda tile: (row, tile))


def call(kernel, tiles, in_specs, out_specs, out_shape, operands, flops, name, **extra):
    shapes = [jax.ShapeDtypeStruct(shape, F32) for shape in out_shape]
    size = sum(4 * o.size for o in operands) + sum(4 * s.size for s in shapes)
    return pl.pallas_call(
        kernel,
        grid=(tiles,),
        in_specs=in_specs,
        out_specs=out_specs,
        out_shape=shapes,
        cost_estimate=pl.CostEstimate(
            flops=int(flops), bytes_accessed=int(size), transcendentals=0
        ),
        compiler_params=pltpu.CompilerParams(vmem_limit_bytes=VMEM_LIMIT),
        name=name,
        **extra,
    )(*operands)


def local(panel, inner_vecs, inner_factor, border_vecs, border_factor, group_start, group_span):
    width = inner_factor.shape[-1]
    height, cols = panel.shape
    steps = inner_factor.shape[1]
    span = cols // TILES
    index = lax.axis_index("row")
    core = lax.axis_index("col")
    active = (index >= group_start) & (index < group_start + group_span)
    flags = jnp.concatenate(
        [
            active.astype(jnp.int32),
            jnp.stack([(index == 0).astype(jnp.int32), core.astype(jnp.int32)]),
        ]
    )
    own_i, own_b = inner_vecs[0], border_vecs[0]
    fac_i, fac_b = inner_factor[0], border_factor[0]

    below = from_behind(panel[:width], "row", -1)
    other_i = other_core(own_i)
    other_b = other_core(own_b)

    square = (2 * width, 2 * width)
    vec = (steps, width, width)
    extra = width * width // cols
    unit = 2 * width * width * cols * 3
    early, bc, up_message = call(
        first_kernel,
        TILES,
        [smem(), whole(vec), whole(vec), whole(vec), columns(width, span, 1), columns(width, span, 2)],
        [whole((2,) + square), columns(2 * width, span), columns(width + extra, span)],
        [(2,) + square, (2 * width, cols), (width + extra, cols)],
        [flags, own_i, other_i, fac_i, panel, panel],
        5 * unit,
        "inner_and_up",
    )
    from_below = from_behind(up_message, "row", -1)
    late, border = call(
        matrix_kernel,
        1,
        [smem()] + [whole(vec)] * 6,
        [whole((2,) + square), whole((steps,) + square)],
        [(2,) + square, (steps,) + square],
        [flags, own_i, other_i, fac_i, own_b, other_b, fac_b],
        6 * unit,
        "matrices",
    )
    down_message, cd = call(
        second_kernel,
        TILES,
        [smem(), columns(width, span, 3), columns(width, span), columns(width, span, 1), whole((2,) + square)],
        [columns(width, span), columns(2 * width, span)],
        [(width, cols), (2 * width, cols)],
        [flags, panel, below, bc, border],
        8 * unit,
        "border_and_down",
    )
    above = from_behind(down_message, "row", 1)
    mixing = from_below[width:].reshape(extra, cols // width, width)
    mixing = mixing.transpose(1, 0, 2).reshape(width, width)
    sent, d = call(
        third_kernel,
        TILES,
        [smem(), columns(width, span), columns(width, span), whole((width, width)), columns(width, span, 1), whole((1,) + square, (2, 0, 0))],
        [columns(width, span), columns(width, span)],
        [(width, cols), (width, cols)],
        [flags, down_message, from_below, mixing, cd, border],
        5 * unit,
        "second_border",
    )
    last = from_behind(sent, "row", 1)
    (out,) = call(
        fourth_kernel,
        TILES,
        [smem(), columns(width, span), columns(width, span), columns(width, span), columns(width, span), columns(width, span), whole((1,) + square, (1, 0, 0)), whole((2,) + square), whole((1,) + square, (3, 0, 0))],
        [columns(height, span)],
        [(height, cols)],
        [flags, panel, above, bc, cd, d, early, late, border],
        16 * unit,
        "rest",
    )
    (out,) = call(
        last_kernel,
        TILES,
        [columns(width, span), whole((1, 2 * width, width), (1, 0, 0)), columns(2 * width, span)],
        [columns(2 * width, span)],
        [(height, cols)],
        [last, late, out],
        2 * unit,
        "finish",
        input_output_aliases={2: 0},
    )
    return out


def solution(mesh):
    placed = (
        P("row", "col"),
        P("row", None, "col", None),
        P("row", None, None, None),
        P("row", None, "col", None),
        P("row", None, None, None),
        P(),
        P(),
    )
    return jax.shard_map(
        local, mesh=mesh, in_specs=placed, out_specs=P("row", "col"), check_vma=False
    )
```

time: 105 us -> 71.8 us (0.68)
  the two profiles are of different devices: /device:TPU:0 before, /device:TPU:12 now
where the time goes in v1:
time: 71.8 us; the launch traced here: 71.4 us
  waiting for transfers between devices  31.6 us (44%)
  Pallas kernels  23 us (32%)
  starting transfers between devices  11.3 us (16%)
  local copies, waits for them, and re-layouts  4.59 us (6%)
  other arithmetic  0.76 us (1%)
    ppermute x4, waiting for transfers between devices, from_behind(): return lax.ppermute(value, axis, pairs)  30.1 us
    pallas_call x6, Pallas kernels, call(): pl.pallas_call(kernel, grid=(tiles,), in_specs=in_specs, out_specs=out_sp...  23 us
    ppermute x4, starting transfers between devices, from_behind(): return lax.ppermute(value, axis, pairs)  11.2 us
    unnamed x12, local copies, waits for them, and re-layouts  3.51 us
    ppermute x2, waiting for transfers between devices, other_core(): lax.ppermute(value, 'col', [(i, (i + 1) % cores) for i in range(cores)])  1.52 us
  transfers between devices with their start and end apart: 6, of which 3 were waited for; matrix products, arithmetic and copies ran while one was open for 3% of the time, Pallas kernels for 27%

profile of v1, /device:TPU:12, one launch (start us, length us, event | category | flops | bytes accessed | tf_op | source)
XLA Modules:
  0.0 71.4 jit_solution(14215721228420149703)
XLA Ops:
  0.0 0.0 collective-permute-start.1
  0.0 1.1 %slice.6 = f32[128,1024]{1,0:T(8,128)S(1)} slice(f32[512,1024]{1,0:T(8,128)} %raw.1), slice={[0:128], [0:1024]} | slice | bytes 1048576 | tf_op jit(solution)/shard_map/slice | solution.py:181
  1.1 3.3 %collective-permute-start = (f32[128,1024]{1,0:T(8,128)S(1)}, f32[128,1024]{1,0:T(8,128)S(1)}, u32[]{:S(2)}, u32[]{:S(2)}) collective-permute-start(f32[128,1024]{1,0:T(8,128)S(1)} %slice.6), channel_id=1, source_target_pairs={{2,0},{4,2},{6,4},{8,6},{10,8},{12,10},{14,12},{16,14},{18,16},{20... | collective-permute-start | bytes 1572872 | tf_op jit(solution)/shard_map/ppermute | solution.py:16
  4.4 0.7 and_convert_fusion
  5.1 0.1 pad_add_fusion.flags
  5.2 0.0 collective-permute-done.1.other.other_i
  5.2 0.0 copy-start
  5.2 1.6 %copy-done = f32[512,1024]{1,0:T(8,128)S(1)} copy-done((f32[512,1024]{1,0:T(8,128)S(1)}, f32[512,1024]{1,0:T(8,128)}, u32[]{:S(2)}) %copy-start) | copy-done | bytes 2097176
  6.8 0.0 copy-start.2
  6.8 0.9 %copy-done.2 = f32[1,4,128,128]{3,2,1,0:T(8,128)S(1)} copy-done((f32[1,4,128,128]{3,2,1,0:T(8,128)S(1)}, f32[1,4,128,128]{3,2,1,0:T(8,128)}, u32[]{:S(2)}) %copy-start.2) | copy-done | bytes 262168
  7.7 0.0 copy-start.3
  7.8 0.9 %copy-done.3 = f32[1,4,128,128]{3,2,1,0:T(8,128)S(1)} copy-done((f32[1,4,128,128]{3,2,1,0:T(8,128)S(1)}, f32[1,4,128,128]{3,2,1,0:T(8,128)}, u32[]{:S(2)}) %copy-start.3) | copy-done | bytes 262168
  8.7 0.0 copy-start.4
  8.7 0.0 copy-start.5
  8.7 4.0 %inner_and_up.1 = (f32[2,256,256]{2,1,0:T(8,128)S(1)}, f32[256,1024]{1,0:T(8,128)S(1)}, f32[144,1024]{1,0:T(8,128)S(1)}) custom-call(s32[6]{0:T(128)S(1)} %pad_add_fusion.flags, f32[4,128,128]{2,1,0:T(8,128)S(1)} %bitcast.15, f32[4,128,128]{2,1,0:T(8,128)S(1)} %collective-permute-done.1.other.other_i, f32[4,128,128]{2,1,0:T(8,128)S(1)} %bitcast.17, ...), custom_call_target="tpu_custom_call" | custom-call | flops 503316480 | bytes 7143448 | tf_op jit(solution)/shard_map/inner_and_up/pallas_call | solution.py:149
  12.7 0.0 copy-start.1
  12.7 2.6 %collective-permute-start.3 = (f32[144,1024]{1,0:T(8,128)S(1)}, f32[144,1024]{1,0:T(8,128)S(1)}, u32[]{:S(2)}, u32[]{:S(2)}) collective-permute-start(f32[144,1024]{1,0:T(8,128)S(1)} %get-tuple-element.17), channel_id=1, source_target_pairs={{2,0},{4,2},{6,4},{8,6},{10,8},{12,10},{14,12},{16,14},{18,16},{20... | collective-permute-start | bytes 1769480 | tf_op jit(solution)/shard_map/ppermute | solution.py:16
  15.3 0.0 copy-done.4
  15.3 0.1 collective-permute-start.2
  15.4 1.5 %collective-permute-done.2.other_b = f32[4,128,128]{2,1,0:T(8,128)S(1)} collective-permute-done((f32[4,128,128]{2,1,0:T(8,128)S(1)}, f32[4,128,128]{2,1,0:T(8,128)S(1)}, u32[]{:S(2)}, u32[]{:S(2)}) %collective-permute-start.2) | collective-permute-done | bytes 262176 | tf_op jit(solution)/shard_map/ppermute | solution.py:21
  16.9 0.0 copy-done.5
  16.9 3.0 %matrices.1 = (f32[2,256,256]{2,1,0:T(8,128)S(1)}, f32[4,256,256]{2,1,0:T(8,128)S(1)}) custom-call(s32[6]{0:T(128)S(1)} %pad_add_fusion.flags, f32[4,128,128]{2,1,0:T(8,128)S(1)} %bitcast.16, f32[4,128,128]{2,1,0:T(8,128)S(1)} %collective-permute-done.1.other.other_i, f32[4,128,128]{2,1,0:T(8,128)S(1)} %bitcast.18, f32[4,128,128]{2,1,0:T(8,128)S(1)} %bitcast.21, ...), custom_call_target="tpu_custom_call" | custom-call | flops 603979776 | bytes 3145752 | tf_op jit(solution)/shard_map/matrices/pallas_call | solution.py:149
  19.9 0.0 collective-permute-done.below
  19.9 0.0 copy-done.1
  19.9 3.4 %border_and_down.1 = (f32[128,1024]{1,0:T(8,128)S(1)}, f32[256,1024]{1,0:T(8,128)S(1)}) custom-call(s32[6]{0:T(128)S(1)} %pad_add_fusion.flags, f32[512,1024]{1,0:T(8,128)S(1)} %copy-done.1, f32[128,1024]{1,0:T(8,128)S(1)} %collective-permute-done.below, f32[256,1024]{1,0:T(8,128)S(1)} %get-tuple-element.14.c.b, f32[4,256,256]{2,1,0:T(8,128)S(1)} %get-tuple-element.15.border), custom_call_target="tpu_custom_call" | custom-call | flops 805306368 | bytes 6291480 | tf_op jit(solution)/shard_map/border_and_down/pallas_call | solution.py:149
  23.3 3.4 %collective-permute-start.5 = (f32[128,1024]{1,0:T(8,128)S(1)}, f32[128,1024]{1,0:T(8,128)S(1)}, u32[]{:S(2)}, u32[]{:S(2)}) collective-permute-start(f32[128,1024]{1,0:T(8,128)S(1)} %get-tuple-element.16.below), channel_id=1, source_target_pairs={{0,2},{2,4},{4,6},{6,8},{8,10},{10,12},{12,14},{14,16},{16,18},{18... | collective-permute-start | bytes 1572872 | tf_op jit(solution)/shard_map/ppermute | solution.py:16
  26.7 25.9 %collective-permute-done.3.message = f32[144,1024]{1,0:T(8,128)S(1)} collective-permute-done((f32[144,1024]{1,0:T(8,128)S(1)}, f32[144,1024]{1,0:T(8,128)S(1)}, u32[]{:S(2)}, u32[]{:S(2)}) %collective-permute-start.3) | collective-permute-done | bytes 589856 | tf_op jit(solution)/shard_map/ppermute | solution.py:16
  52.7 2.9 %second_border.1 = (f32[128,1024]{1,0:T(8,128)S(1)}, f32[128,1024]{1,0:T(8,128)S(1)}) custom-call(s32[6]{0:T(128)S(1)} %pad_add_fusion.flags, f32[128,1024]{1,0:T(8,128)S(1)} %get-tuple-element.16.below, f32[144,1024]{1,0:T(8,128)S(1)} %collective-permute-done.3.message, f32[128,128]{1,0:T(8,128)S(1)} %bitcast.19, f32[256,1024]{1,0:T(8,128)S(1)} %get-tuple-element.18.d.c, ...), custom_call_target="tpu_custom_call" | custom-call | flops 503316480 | bytes 4325400 | tf_op jit(solution)/shard_map/second_border/pallas_call | solution.py:149
  55.6 1.9 %collective-permute-start.4 = (f32[128,1024]{1,0:T(8,128)S(1)}, f32[128,1024]{1,0:T(8,128)S(1)}, u32[]{:S(2)}, u32[]{:S(2)}) collective-permute-start(f32[128,1024]{1,0:T(8,128)S(1)} %get-tuple-element.19), channel_id=1, source_target_pairs={{0,2},{2,4},{4,6},{6,8},{8,10},{10,12},{12,14},{14,16},{16,18},{18... | collective-permute-start | bytes 1572872 | tf_op jit(solution)/shard_map/ppermute | solution.py:16
  57.5 0.0 collective-permute-done.5.above
  57.5 5.9 %rest.1.before = f32[512,1024]{1,0:T(8,128)} custom-call(s32[6]{0:T(128)S(1)} %pad_add_fusion.flags, f32[512,1024]{1,0:T(8,128)S(1)} %copy-done.1, f32[128,1024]{1,0:T(8,128)S(1)} %collective-permute-done.5.above, f32[256,1024]{1,0:T(8,128)S(1)} %get-tuple-element.14.c.b, f32[256,1024]{1,0:T(8,128)S(1)} %get-tuple-element.18.d.c, ...), custom_call_target="tpu_custom_call" | custom-call | flops 1610612736 | bytes 9437208 | tf_op jit(solution)/shard_map/rest/pallas_call | solution.py:149
  63.4 4.2 %collective-permute-done.4.above = f32[128,1024]{1,0:T(8,128)S(1)} collective-permute-done((f32[128,1024]{1,0:T(8,128)S(1)}, f32[128,1024]{1,0:T(8,128)S(1)}, u32[]{:S(2)}, u32[]{:S(2)}) %collective-permute-start.4) | collective-permute-done | bytes 524320 | tf_op jit(solution)/shard_map/ppermute | solution.py:16
  67.5 3.9 %finish.1 = f32[512,1024]{1,0:T(8,128)} custom-call(f32[128,1024]{1,0:T(8,128)S(1)} %collective-permute-done.4.above, f32[2,256,256]{2,1,0:T(8,128)S(1)} %get-tuple-element.20.late, f32[512,1024]{1,0:T(8,128)} %rest.1.before), custom_call_target="tpu_custom_call", output_to_operand_aliasing={{}: (2, {})} | custom-call | flops 201326592 | bytes 5242880 | tf_op jit(solution)/shard_map/finish/pallas_call | solution.py:149
  (1 shorter events, 0.0 us)
Async XLA Ops:
  0.0 5.2 %collective-permute-start.1 = (f32[4,128,128]{2,1,0:T(8,128)}, f32[4,128,128]{2,1,0:T(8,128)S(1)}, u32[]{:S(2)}, u32[]{:S(2)}) collective-permute-start(f32[4,128,128]{2,1,0:T(8,128)} %bitcast.14), channel_id=1, source_target_pairs={{0,1},{1,0},{2,3},{3,2},{4,5},{5,4},{6,7},{7,6},{8,9},{9,8},{10,11... | collective-permute-start | bytes 786440 | tf_op jit(solution)/shard_map/ppermute | solution.py:21
  1.1 18.8 %collective-permute-start = (f32[128,1024]{1,0:T(8,128)S(1)}, f32[128,1024]{1,0:T(8,128)S(1)}, u32[]{:S(2)}, u32[]{:S(2)}) collective-permute-start(f32[128,1024]{1,0:T(8,128)S(1)} %slice.6), channel_id=1, source_target_pairs={{2,0},{4,2},{6,4},{8,6},{10,8},{12,10},{14,12},{16,14},{18,16},{20... | collective-permute-start | bytes 1572872 | tf_op jit(solution)/shard_map/ppermute | solution.py:16
  5.2 1.6 %copy-start = (f32[512,1024]{1,0:T(8,128)S(1)}, f32[512,1024]{1,0:T(8,128)}, u32[]{:S(2)}) copy-start(f32[512,1024]{1,0:T(8,128)} %raw.1) | copy-start | bytes 6291460
  6.8 0.9 %copy-start.2 = (f32[1,4,128,128]{3,2,1,0:T(8,128)S(1)}, f32[1,4,128,128]{3,2,1,0:T(8,128)}, u32[]{:S(2)}) copy-start(f32[1,4,128,128]{3,2,1,0:T(8,128)} %param.8) | copy-start | bytes 786436
  7.7 0.9 %copy-start.3 = (f32[1,4,128,128]{3,2,1,0:T(8,128)S(1)}, f32[1,4,128,128]{3,2,1,0:T(8,128)}, u32[]{:S(2)}) copy-start(f32[1,4,128,128]{3,2,1,0:T(8,128)} %param.9) | copy-start | bytes 786436
  8.7 6.6 %copy-start.4 = (f32[1,4,128,128]{3,2,1,0:T(8,128)S(1)}, f32[1,4,128,128]{3,2,1,0:T(8,128)}, u32[]{:S(2)}) copy-start(f32[1,4,128,128]{3,2,1,0:T(8,128)} %param.10) | copy-start | bytes 786436
  8.7 8.2 %copy-start.5 = (f32[1,4,128,128]{3,2,1,0:T(8,128)S(1)}, f32[1,4,128,128]{3,2,1,0:T(8,128)}, u32[]{:S(2)}) copy-start(f32[1,4,128,128]{3,2,1,0:T(8,128)} %param.11) | copy-start | bytes 786436
  12.7 7.2 %copy-start.1 = (f32[512,1024]{1,0:T(8,128)S(1)}, f32[512,1024]{1,0:T(8,128)}, u32[]{:S(2)}) copy-start(f32[512,1024]{1,0:T(8,128)} %raw.1) | copy-start | bytes 6291460
  12.7 40.0 %collective-permute-start.3 = (f32[144,1024]{1,0:T(8,128)S(1)}, f32[144,1024]{1,0:T(8,128)S(1)}, u32[]{:S(2)}, u32[]{:S(2)}) collective-permute-start(f32[144,1024]{1,0:T(8,128)S(1)} %get-tuple-element.17), channel_id=1, source_target_pairs={{2,0},{4,2},{6,4},{8,6},{10,8},{12,10},{14,12},{16,14},{18,16},{20... | collective-permute-start | bytes 1769480 | tf_op jit(solution)/shard_map/ppermute | solution.py:16
  15.3 1.6 %collective-permute-start.2 = (f32[4,128,128]{2,1,0:T(8,128)S(1)}, f32[4,128,128]{2,1,0:T(8,128)S(1)}, u32[]{:S(2)}, u32[]{:S(2)}) collective-permute-start(f32[4,128,128]{2,1,0:T(8,128)S(1)} %bitcast.20), channel_id=1, source_target_pairs={{0,1},{1,0},{2,3},{3,2},{4,5},{5,4},{6,7},{7,6},{8,9},{9,8},{10,11... | collective-permute-start | bytes 786440 | tf_op jit(solution)/shard_map/ppermute | solution.py:21
  23.3 34.2 %collective-permute-start.5 = (f32[128,1024]{1,0:T(8,128)S(1)}, f32[128,1024]{1,0:T(8,128)S(1)}, u32[]{:S(2)}, u32[]{:S(2)}) collective-permute-start(f32[128,1024]{1,0:T(8,128)S(1)} %get-tuple-element.16.below), channel_id=1, source_target_pairs={{0,2},{2,4},{4,6},{6,8},{8,10},{10,12},{12,14},{14,16},{16,18},{18... | collective-permute-start | bytes 1572872 | tf_op jit(solution)/shard_map/ppermute | solution.py:16
  55.6 12.0 %collective-permute-start.4 = (f32[128,1024]{1,0:T(8,128)S(1)}, f32[128,1024]{1,0:T(8,128)S(1)}, u32[]{:S(2)}, u32[]{:S(2)}) collective-permute-start(f32[128,1024]{1,0:T(8,128)S(1)} %get-tuple-element.19), channel_id=1, source_target_pairs={{0,2},{2,4},{4,6},{6,8},{8,10},{10,12},{12,14},{14,16},{16,18},{18... | collective-permute-start | bytes 1572872 | tf_op jit(solution)/shard_map/ppermute | solution.py:16

commit v2 on v1

v2 whole, which is shorter than its diff:
```python
import functools

import jax
import jax.numpy as jnp
from jax import lax
from jax.experimental import pallas as pl
from jax.experimental.pallas import tpu as pltpu
from jax.sharding import PartitionSpec as P

F32 = jnp.float32
TILES = 2
EIGHTHS_UP = (4, 4)
EIGHTHS_DOWN = (4, 4)
VMEM_LIMIT = 24 * 1024 * 1024


def from_behind(value, axis, by):
    devices = lax.axis_size(axis)
    pairs = [(i, i + by) for i in range(devices) if 0 <= i + by < devices]
    return lax.ppermute(value, axis, pairs)


def other_core(value):
    cores = lax.axis_size("col")
    return lax.ppermute(value, "col", [(i, (i + 1) % cores) for i in range(cores)])


def split(x):
    high = x.astype(jnp.bfloat16)
    return high, (x - high.astype(F32)).astype(jnp.bfloat16)


def dot(x, y, contract=(1, 0)):
    def product(left, right):
        return lax.dot_general(
            left,
            right,
            (((contract[0],), (contract[1],)), ((), ())),
            preferred_element_type=F32,
        )

    xh, xl = split(x)
    yh, yl = split(y)
    return product(xl, yh) + product(xh, yl) + product(xh, yh)


def change_of(first, second, factor, core):
    upper = jnp.where(core == 0, first, second)
    lower = jnp.where(core == 0, second, first)
    vectors = jnp.concatenate([upper, lower], axis=0)
    return dot(dot(vectors, factor), vectors, (1, 1))


def stacked(upper, lower):
    return jnp.concatenate([upper, lower], axis=0)


def is_active(starts, spans, step):
    index = lax.axis_index("row")
    return (index >= starts[step]) & (index < starts[step] + spans[step])


def pieces(cols, eighths):
    ends = [cols * sum(eighths[:at]) // 8 for at in range(len(eighths) + 1)]
    return [slice(a, b) for a, b in zip(ends[:-1], ends[1:])]


def first_kernel(own, other, factor, panel, early, bc, *rest):
    *messages, vectors, factors, band, sems = rest
    width = factor.shape[-1]
    parts = pieces(panel.shape[1], EIGHTHS_UP)
    copies = [
        pltpu.make_async_copy(own.at[pl.ds(0, 2)], vectors, sems.at[0]),
        pltpu.make_async_copy(factor.at[pl.ds(0, 2)], factors, sems.at[1]),
    ] + [
        pltpu.make_async_copy(
            panel.at[pl.ds(width, 2 * width), part], band.at[:, part], sems.at[2 + at]
        )
        for at, part in enumerate(parts)
    ]
    for copy in copies:
        copy.start()
    copies[0].wait()
    copies[1].wait()
    core = lax.axis_index("col")
    for step in range(2):
        early[step] = change_of(vectors[step], other[step], factors[step], core)
    last = messages[-1]
    extra = last.shape[0] - width
    for block in range(last.shape[1] // width):
        last[width:, block * width : (block + 1) * width] = early[
            1, block * extra : (block + 1) * extra, :width
        ]
    for at, part in enumerate(parts):
        copies[2 + at].wait()
        tall = band[:, part]
        tall = tall - dot(early[0], tall)
        bc[:, part] = tall
        messages[at][:width] = dot(early[1, :width, width:], tall[:width])


def matrix_kernel(own_i, other_i, fac_i, own_b, other_b, fac_b, late, border):
    core = lax.axis_index("col")
    for step in range(late.shape[0]):
        late[step] = change_of(own_i[step], other_i[step], fac_i[step], core)
    for step in range(border.shape[0]):
        border[step] = change_of(own_b[step], other_b[step], fac_b[step], core)


def second_kernel(starts, spans, d, below, c, border, message, cd):
    width = d.shape[0]
    band = stacked(d[...], below[...])
    band = jnp.where(is_active(starts, spans, 0), band - dot(border[0], band), band)
    message[...] = band[width:]
    band = stacked(c[...], band[:width])
    cd[...] = jnp.where(is_active(starts, spans, 1), band - dot(border[1], band), band)


def third_kernel(starts, spans, below, cd, border, *rest):
    count = len(EIGHTHS_UP)
    messages, d_out, sent = rest[:count], rest[count], rest[count + 1 :]
    width, cols = d_out.shape
    cuts = pieces(cols, EIGHTHS_DOWN)
    last = messages[-1]
    mixing = jnp.concatenate(
        [
            last[width:, block * width : (block + 1) * width]
            for block in range(last.shape[1] // width)
        ],
        axis=0,
    )
    for message, part in zip(messages, pieces(cols, EIGHTHS_UP)):
        low = below[:, part]
        low = low - dot(mixing, low) - message[:width]
        band = stacked(cd[width:, part], low)
        band = jnp.where(is_active(starts, spans, 2), band - dot(border[0], band), band)
        d_out[:, part] = band[:width]
        for cut, out in zip(cuts, sent):
            a, b = max(cut.start, part.start), min(cut.stop, part.stop)
            if a < b:
                out[:, a - cut.start : b - cut.start] = band[
                    width:, a - part.start : b - part.start
                ]


def fourth_kernel(starts, spans, raw, above, bc, cd, d, second, late, border, out, before, held, sems):
    width, cols = raw.shape
    span = cols // TILES
    first = lax.axis_index("row") == 0
    copies = []
    for part in range(TILES):
        here = slice(part * span, (part + 1) * span)
        ab = stacked(jnp.where(first, raw[:, here], above[:, here]), bc[:width, here])
        ab = ab - dot(second[0], ab)
        low = stacked(ab[width:], cd[:width, here])
        low = low - dot(late[0], low)
        end = stacked(low[width:], d[:, here])
        held[:, here] = jnp.where(is_active(starts, spans, 3), end - dot(border[0], end), end)
        copy = pltpu.make_async_copy(
            held.at[:, pl.ds(part * span, span)],
            out.at[pl.ds(2 * width, 2 * width), pl.ds(part * span, span)],
            sems.at[part],
        )
        copy.start()
        copies.append(copy)
        ab = stacked(jnp.where(first, ab[:width], 0.0), low[:width])
        before[:, here] = ab - dot(late[1], ab)
    for copy in copies:
        copy.wait()


def last_kernel(cut, above, late, before, out_in, out, held, sem):
    del out_in
    width = above.shape[0]
    top = above[...]
    change = dot(late[0], top)
    held[:width] = before[:width, cut] + (top - change[:width])
    held[width:] = before[width:, cut] - change[width:]
    copy = pltpu.make_async_copy(held, out.at[pl.ds(0, 2 * width), cut], sem)
    copy.start()
    copy.wait()


def smem():
    return pl.BlockSpec(memory_space=pltpu.SMEM)


def hbm():
    return pl.BlockSpec(memory_space=pltpu.HBM)


def whole(shape, index=None):
    index = (0,) * len(shape) if index is None else index
    return pl.BlockSpec(shape, lambda tile: index)


def columns(rows, span, row=0):
    return pl.BlockSpec((rows, span), lambda tile: (row, tile))


def call(kernel, tiles, in_specs, out_specs, out_shape, operands, name, vmem=VMEM_LIMIT, **extra):
    shapes = [jax.ShapeDtypeStruct(shape, F32) for shape in out_shape]
    return pl.pallas_call(
        kernel,
        grid=(tiles,),
        in_specs=in_specs,
        out_specs=out_specs,
        out_shape=shapes,
        cost_estimate=pl.CostEstimate(flops=1, bytes_accessed=1, transcendentals=0),
        compiler_params=pltpu.CompilerParams(vmem_limit_bytes=vmem),
        name=name,
        **extra,
    )(*operands)


def local(panel, inner_vecs, inner_factor, border_vecs, border_factor, group_start, group_span):
    width = inner_factor.shape[-1]
    height, cols = panel.shape
    steps = inner_factor.shape[1]
    span = cols // TILES
    own_i, own_b = inner_vecs[0], border_vecs[0]
    fac_i, fac_b = inner_factor[0], border_factor[0]

    below = from_behind(panel[:width], "row", -1)
    other_i = other_core(own_i)
    other_b = other_core(own_b)

    square = (2 * width, 2 * width)
    vec = (steps, width, width)
    ups = [part.stop - part.start for part in pieces(cols, EIGHTHS_UP)]
    cuts = pieces(cols, EIGHTHS_DOWN)
    downs = [cut.stop - cut.start for cut in cuts]
    extra = width * width // ups[-1]
    shapes = [(width, up) for up in ups[:-1]] + [(width + extra, ups[-1])]
    early, bc, *up_messages = call(
        first_kernel,
        1,
        [hbm(), whole((2, width, width)), hbm(), hbm()],
        [whole((2,) + square), whole((2 * width, cols))] + [whole(shape) for shape in shapes],
        [(2,) + square, (2 * width, cols)] + shapes,
        [own_i[:2], other_i, fac_i[:2], panel],
        "inner_and_up",
        vmem=50 * 1024 * 1024,
        scratch_shapes=[
            pltpu.VMEM((2, width, width), F32),
            pltpu.VMEM((2, width, width), F32),
            pltpu.VMEM((2 * width, cols), F32),
            pltpu.SemaphoreType.DMA((2 + len(ups),)),
        ],
    )
    from_below = [from_behind(message, "row", -1) for message in up_messages]
    below, from_below[0] = lax.optimization_barrier((below, from_below[0]))
    late, border = call(
        matrix_kernel,
        1,
        [whole((2, width, width), (1, 0, 0))] * 3 + [whole(vec)] * 3,
        [whole((2,) + square), whole((steps,) + square)],
        [(2,) + square, (steps,) + square],
        [own_i, other_i, fac_i, own_b, other_b, fac_b],
        "matrices",
    )
    down_message, cd = call(
        second_kernel,
        TILES,
        [smem(), smem(), columns(width, span, 3), columns(width, span), columns(width, span, 1), whole((2,) + square)],
        [columns(width, span), columns(2 * width, span)],
        [(width, cols), (2 * width, cols)],
        [group_start, group_span, panel, below, bc, border],
        "border_and_down",
    )
    above = from_behind(down_message, "row", 1)
    d, *sent = call(
        third_kernel,
        1,
        [smem(), smem(), whole((width, cols)), whole((2 * width, cols)), whole((1,) + square, (2, 0, 0))] + [whole(shape) for shape in shapes],
        [whole((width, cols))] + [whole((width, down)) for down in downs],
        [(width, cols)] + [(width, down) for down in downs],
        [group_start, group_span, down_message, cd, border] + from_below,
        "second_border",
    )
    last = [from_behind(part, "row", 1) for part in sent]
    out, before = call(
        fourth_kernel,
        1,
        [smem(), smem(), whole((width, cols)), whole((width, cols)), whole((2 * width, cols)), whole((2 * width, cols)), whole((width, cols)), whole((1,) + square, (1, 0, 0)), whole((2,) + square), whole((1,) + square, (3, 0, 0))],
        [pl.BlockSpec(memory_space=pl.ANY), whole((2 * width, cols))],
        [(height, cols), (2 * width, cols)],
        [group_start, group_span, panel, above, bc, cd, d, early, late, border],
        "rest",
        scratch_shapes=[pltpu.VMEM((2 * width, cols), F32), pltpu.SemaphoreType.DMA((TILES,))],
    )
    for cut, down, part in zip(cuts, downs, last):
        (out,) = call(
            functools.partial(last_kernel, cut),
            1,
            [whole((width, down)), whole((1, 2 * width, width), (1, 0, 0)), whole((2 * width, cols)), pl.BlockSpec(memory_space=pl.ANY)],
            [pl.BlockSpec(memory_space=pl.ANY)],
            [(height, cols)],
            [part, late, before, out],
            "finish",
            scratch_shapes=[pltpu.VMEM((2 * width, down), F32), pltpu.SemaphoreType.DMA],
            input_output_aliases={3: 0},
        )
    return out


def solution(mesh):
    placed = (
        P("row", "col"),
        P("row", None, "col", None),
        P("row", None, None, None),
        P("row", None, "col", None),
        P("row", None, None, None),
        P(),
        P(),
    )
    return jax.shard_map(
        local, mesh=mesh, in_specs=placed, out_specs=P("row", "col"), check_vma=False
    )
```

time: 71.8 us -> 56.3 us (0.78)
  the two profiles are of different devices: /device:TPU:12 before, /device:TPU:0 now
where the time goes in v2:
time: 56.3 us; the launch traced here: 56 us
  waiting for transfers between devices  22.4 us (40%)
  starting transfers between devices  17 us (30%)
  Pallas kernels  14.3 us (25%)
  local copies, waits for them, and re-layouts  2.09 us (4%)
    ppermute x6, waiting for transfers between devices, from_behind(): return lax.ppermute(value, axis, pairs)  22.4 us
    ppermute x6, starting transfers between devices, from_behind(): return lax.ppermute(value, axis, pairs)  16.3 us
    pallas_call x7, Pallas kernels, call(): pl.pallas_call(kernel, grid=(tiles,), in_specs=in_specs, out_specs=out_sp...  14.3 us
  transfers between devices with their start and end apart: 8, of which 5 were waited for; matrix products, arithmetic and copies ran while one was open for 4% of the time, Pallas kernels for 23%

profile of v2, /device:TPU:0, one launch (start us, length us, event | category | flops | bytes accessed | tf_op | source)
XLA Modules:
  0.0 56.0 jit_solution(13601048109829218600)
XLA Ops:
  0.0 0.0 copy-start.1
  0.0 0.0 copy-start.2
  0.0 0.0 copy-start.3
  0.0 0.0 copy-start.4
  0.0 0.5 collective-permute-start.1
  0.5 1.1 %slice.15 = f32[128,1024]{1,0:T(8,128)S(1)} slice(f32[512,1024]{1,0:T(8,128)} %raw.1), slice={[0:128], [0:1024]} | slice | bytes 1048576 | tf_op jit(solution)/shard_map/slice | solution.py:224
  1.6 1.3 %collective-permute-start = (f32[128,1024]{1,0:T(8,128)S(1)}, f32[128,1024]{1,0:T(8,128)S(1)}, u32[]{:S(2)}, u32[]{:S(2)}) collective-permute-start(f32[128,1024]{1,0:T(8,128)S(1)} %slice.15), channel_id=1, source_target_pairs={{2,0},{4,2},{6,4},{8,6},{10,8},{12,10},{14,12},{16,14},{18,16},{20... | collective-permute-start | bytes 1572872 | tf_op jit(solution)/shard_map/ppermute | solution.py:20
  2.9 0.2 collective-permute-start.3
  3.1 1.0 %slice_bitcast_fusion = (f32[2,128,128]{2,1,0:T(8,128)S(1)}, f32[2,128,128]{2,1,0:T(8,128)S(1)}) fusion(f32[1,4,128,128]{3,2,1,0:T(8,128)} %param.9, f32[1,4,128,128]{3,2,1,0:T(8,128)} %param.8), kind=kLoop, calls=%fused_computation | loop fusion | bytes 524288 | tf_op jit(solution)/shard_map/slice | solution.py:241
  4.1 0.0 collective-permute-done.1.other.other_i
  4.1 0.0 copy-start
  4.1 0.0 copy-start.5
  4.1 0.0 copy-start.6
  4.1 3.0 %inner_and_up.1 = (f32[2,256,256]{2,1,0:T(8,128)S(1)}, f32[256,1024]{1,0:T(8,128)S(1)}, f32[128,512]{1,0:T(8,128)S(1)}, f32[160,512]{1,0:T(8,128)S(1)}) custom-call(f32[2,128,128]{2,1,0:T(8,128)S(1)} %get-tuple-element.36.own, f32[4,128,128]{2,1,0:T(8,128)S(1)} %collective-permute-done.1.other.other_i, f32[2,128,128]{2,1,0:T(8,128)S(1)} %get-tuple-element.35.factor, ...), custom_call_target="tpu_custom_call" | custom-call | flops 1 | bytes 1 | tf_op jit(solution)/shard_map/inner_and_up/pallas_call | solution.py:203
  7.2 1.3 %collective-permute-start.2 = (f32[128,512]{1,0:T(8,128)S(1)}, f32[128,512]{1,0:T(8,128)S(1)}, u32[]{:S(2)}, u32[]{:S(2)}) collective-permute-start(f32[128,512]{1,0:T(8,128)S(1)} %get-tuple-element.20), channel_id=1, source_target_pairs={{2,0},{4,2},{6,4},{8,6},{10,8},{12,10},{14,12},{16,14},{18,16},{20... | collective-permute-start | bytes 786440 | tf_op jit(solution)/shard_map/ppermute | solution.py:20
  8.5 1.3 %collective-permute-start.4 = (f32[160,512]{1,0:T(8,128)S(1)}, f32[160,512]{1,0:T(8,128)S(1)}, u32[]{:S(2)}, u32[]{:S(2)}) collective-permute-start(f32[160,512]{1,0:T(8,128)S(1)} %get-tuple-element.27), channel_id=1, source_target_pairs={{2,0},{4,2},{6,4},{8,6},{10,8},{12,10},{14,12},{16,14},{18,16},{20... | collective-permute-start | bytes 983048 | tf_op jit(solution)/shard_map/ppermute | solution.py:20
  9.8 0.0 collective-permute-done.3.other_b
  9.8 0.0 copy-done.1
  9.8 0.0 copy-done.2
  9.8 0.0 copy-done.3
  9.8 0.0 copy-done.4
  9.8 1.4 %matrices.1 = (f32[2,256,256]{2,1,0:T(8,128)S(1)}, f32[4,256,256]{2,1,0:T(8,128)S(1)}) custom-call(f32[4,128,128]{2,1,0:T(8,128)S(1)} %bitcast.10, f32[4,128,128]{2,1,0:T(8,128)S(1)} %collective-permute-done.1.other.other_i, f32[4,128,128]{2,1,0:T(8,128)S(1)} %bitcast.8, f32[4,128,128]{2,1,0:T(8,128)S(1)} %bitcast.12, ...), custom_call_target="tpu_custom_call" | custom-call | flops 1 | bytes 1 | tf_op jit(solution)/shard_map/matrices/pallas_call | solution.py:203
  11.2 7.7 %collective-permute-done.below = f32[128,1024]{1,0:T(8,128)S(1)} collective-permute-done((f32[128,1024]{1,0:T(8,128)S(1)}, f32[128,1024]{1,0:T(8,128)S(1)}, u32[]{:S(2)}, u32[]{:S(2)}) %collective-permute-start) | collective-permute-done | bytes 524320 | tf_op jit(solution)/shard_map/ppermute | solution.py:20
  18.9 5.6 %collective-permute-done.2.rest_0_ = f32[128,512]{1,0:T(8,128)S(1)} collective-permute-done((f32[128,512]{1,0:T(8,128)S(1)}, f32[128,512]{1,0:T(8,128)S(1)}, u32[]{:S(2)}, u32[]{:S(2)}) %collective-permute-start.2) | collective-permute-done | bytes 262176 | tf_op jit(solution)/shard_map/ppermute | solution.py:20
  24.5 0.0 copy-done
  24.5 0.0 copy-done.5
  24.5 0.0 copy-done.6
  24.5 2.2 %border_and_down.1 = (f32[128,1024]{1,0:T(8,128)S(1)}, f32[256,1024]{1,0:T(8,128)S(1)}) custom-call(s32[4]{0:T(128)S(1)} %copy-done.5, s32[4]{0:T(128)S(1)} %copy-done.6, f32[512,1024]{1,0:T(8,128)S(1)} %copy-done, f32[128,1024]{1,0:T(8,128)S(1)} %collective-permute-done.below, f32[256,1024]{1,0:T(8,128)S(1)} %get-tuple-element.22.c.bc, ...), custom_call_target="tpu_custom_call" | custom-call | flops 1 | bytes 1 | tf_op jit(solution)/shard_map/border_and_down/pallas_call | solution.py:203
  26.7 4.8 %collective-permute-start.6 = (f32[128,1024]{1,0:T(8,128)S(1)}, f32[128,1024]{1,0:T(8,128)S(1)}, u32[]{:S(2)}, u32[]{:S(2)}) collective-permute-start(f32[128,1024]{1,0:T(8,128)S(1)} %get-tuple-element.24.below), channel_id=1, source_target_pairs={{0,2},{2,4},{4,6},{6,8},{8,10},{10,12},{12,14},{14,16},{16,18},{18... | collective-permute-start | bytes 1572872 | tf_op jit(solution)/shard_map/ppermute | solution.py:20
  31.5 0.0 collective-permute-done.4.rest_1_
  31.5 1.6 %second_border.1 = (f32[128,1024]{1,0:T(8,128)S(1)}, f32[128,512]{1,0:T(8,128)S(1)}, f32[128,512]{1,0:T(8,128)S(1)}) custom-call(s32[4]{0:T(128)S(1)} %copy-done.5, s32[4]{0:T(128)S(1)} %copy-done.6, f32[128,1024]{1,0:T(8,128)S(1)} %get-tuple-element.24.below, f32[256,1024]{1,0:T(8,128)S(1)} %get-tuple-element.25.cd, ...), custom_call_target="tpu_custom_call" | custom-call | flops 1 | bytes 1 | tf_op jit(solution)/shard_map/second_border/pallas_call | solution.py:203
  33.1 4.3 %collective-permute-start.7 = (f32[128,512]{1,0:T(8,128)S(1)}, f32[128,512]{1,0:T(8,128)S(1)}, u32[]{:S(2)}, u32[]{:S(2)}) collective-permute-start(f32[128,512]{1,0:T(8,128)S(1)} %get-tuple-element.33), channel_id=1, source_target_pairs={{0,2},{2,4},{4,6},{6,8},{8,10},{10,12},{12,14},{14,16},{16,18},{18... | collective-permute-start | bytes 786440 | tf_op jit(solution)/shard_map/ppermute | solution.py:20
  37.5 3.4 %collective-permute-start.5 = (f32[128,512]{1,0:T(8,128)S(1)}, f32[128,512]{1,0:T(8,128)S(1)}, u32[]{:S(2)}, u32[]{:S(2)}) collective-permute-start(f32[128,512]{1,0:T(8,128)S(1)} %get-tuple-element.28), channel_id=1, source_target_pairs={{0,2},{2,4},{4,6},{6,8},{8,10},{10,12},{12,14},{14,16},{16,18},{18... | collective-permute-start | bytes 786440 | tf_op jit(solution)/shard_map/ppermute | solution.py:20
  40.8 2.9 %collective-permute-done.6.above = f32[128,1024]{1,0:T(8,128)S(1)} collective-permute-done((f32[128,1024]{1,0:T(8,128)S(1)}, f32[128,1024]{1,0:T(8,128)S(1)}, u32[]{:S(2)}, u32[]{:S(2)}) %collective-permute-start.6) | collective-permute-done | bytes 524320 | tf_op jit(solution)/shard_map/ppermute | solution.py:20
  43.8 3.7 %rest.1 = (f32[512,1024]{1,0:T(8,128)}, f32[256,1024]{1,0:T(8,128)S(1)}) custom-call(s32[4]{0:T(128)S(1)} %copy-done.5, s32[4]{0:T(128)S(1)} %copy-done.6, f32[512,1024]{1,0:T(8,128)S(1)} %copy-done, f32[128,1024]{1,0:T(8,128)S(1)} %collective-permute-done.6.above, f32[256,1024]{1,0:T(8,128)S(1)} %get-tuple-element.22.c.bc, ...), custom_call_target="tpu_custom_call" | custom-call | flops 1 | bytes 1 | tf_op jit(solution)/shard_map/rest/pallas_call | solution.py:203
  47.5 1.9 %collective-permute-done.7.above = f32[128,512]{1,0:T(8,128)S(1)} collective-permute-done((f32[128,512]{1,0:T(8,128)S(1)}, f32[128,512]{1,0:T(8,128)S(1)}, u32[]{:S(2)}, u32[]{:S(2)}) %collective-permute-start.7) | collective-permute-done | bytes 262176 | tf_op jit(solution)/shard_map/ppermute | solution.py:20
  49.4 1.2 %finish.2.out_in = f32[512,1024]{1,0:T(8,128)} custom-call(f32[128,512]{1,0:T(8,128)S(1)} %collective-permute-done.7.above, f32[2,256,256]{2,1,0:T(8,128)S(1)} %get-tuple-element.29.late, f32[256,1024]{1,0:T(8,128)S(1)} %get-tuple-element.32.before, f32[512,1024]{1,0:T(8,128)} %get-tuple-element.34.out_in), custom_call_target="tpu_custom_call", output_to_operand_aliasing={{}: (3, {})} | custom-call | flops 1 | bytes 1 | tf_op jit(solution)/shard_map/finish/pallas_call | solution.py:203
  50.5 4.3 %collective-permute-done.5.above = f32[128,512]{1,0:T(8,128)S(1)} collective-permute-done((f32[128,512]{1,0:T(8,128)S(1)}, f32[128,512]{1,0:T(8,128)S(1)}, u32[]{:S(2)}, u32[]{:S(2)}) %collective-permute-start.5) | collective-permute-done | bytes 262176 | tf_op jit(solution)/shard_map/ppermute | solution.py:20
  54.8 1.2 %finish.3 = f32[512,1024]{1,0:T(8,128)} custom-call(f32[128,512]{1,0:T(8,128)S(1)} %collective-permute-done.5.above, f32[2,256,256]{2,1,0:T(8,128)S(1)} %get-tuple-element.29.late, f32[256,1024]{1,0:T(8,128)S(1)} %get-tuple-element.32.before, f32[512,1024]{1,0:T(8,128)} %finish.2.out_in), custom_call_target="tpu_custom_call", output_to_operand_aliasing={{}: (3, {})} | custom-call | flops 1 | bytes 1 | tf_op jit(solution)/shard_map/finish/pallas_call | solution.py:203
Async XLA Ops:
  0.0 9.8 %copy-start.1 = (f32[1,4,128,128]{3,2,1,0:T(8,128)S(1)}, f32[1,4,128,128]{3,2,1,0:T(8,128)}, u32[]{:S(2)}) copy-start(f32[1,4,128,128]{3,2,1,0:T(8,128)} %param.9) | copy-start | bytes 786436
  0.0 9.8 %copy-start.2 = (f32[1,4,128,128]{3,2,1,0:T(8,128)S(1)}, f32[1,4,128,128]{3,2,1,0:T(8,128)}, u32[]{:S(2)}) copy-start(f32[1,4,128,128]{3,2,1,0:T(8,128)} %param.8) | copy-start | bytes 786436
  0.0 9.8 %copy-start.3 = (f32[1,4,128,128]{3,2,1,0:T(8,128)S(1)}, f32[1,4,128,128]{3,2,1,0:T(8,128)}, u32[]{:S(2)}) copy-start(f32[1,4,128,128]{3,2,1,0:T(8,128)} %param.10) | copy-start | bytes 786436
  0.0 9.8 %copy-start.4 = (f32[1,4,128,128]{3,2,1,0:T(8,128)S(1)}, f32[1,4,128,128]{3,2,1,0:T(8,128)}, u32[]{:S(2)}) copy-start(f32[1,4,128,128]{3,2,1,0:T(8,128)} %param.11) | copy-start | bytes 786436
  0.0 4.1 %collective-permute-start.1 = (f32[4,128,128]{2,1,0:T(8,128)}, f32[4,128,128]{2,1,0:T(8,128)S(1)}, u32[]{:S(2)}, u32[]{:S(2)}) collective-permute-start(f32[4,128,128]{2,1,0:T(8,128)} %bitcast.9), channel_id=1, source_target_pairs={{0,1},{1,0},{2,3},{3,2},{4,5},{5,4},{6,7},{7,6},{8,9},{9,8},{10,11... | collective-permute-start | bytes 786440 | tf_op jit(solution)/shard_map/ppermute | solution.py:25
  1.6 17.2 %collective-permute-start = (f32[128,1024]{1,0:T(8,128)S(1)}, f32[128,1024]{1,0:T(8,128)S(1)}, u32[]{:S(2)}, u32[]{:S(2)}) collective-permute-start(f32[128,1024]{1,0:T(8,128)S(1)} %slice.15), channel_id=1, source_target_pairs={{2,0},{4,2},{6,4},{8,6},{10,8},{12,10},{14,12},{16,14},{18,16},{20... | collective-permute-start | bytes 1572872 | tf_op jit(solution)/shard_map/ppermute | solution.py:20
  2.9 6.8 %collective-permute-start.3 = (f32[4,128,128]{2,1,0:T(8,128)}, f32[4,128,128]{2,1,0:T(8,128)S(1)}, u32[]{:S(2)}, u32[]{:S(2)}) collective-permute-start(f32[4,128,128]{2,1,0:T(8,128)} %bitcast.11), channel_id=1, source_target_pairs={{0,1},{1,0},{2,3},{3,2},{4,5},{5,4},{6,7},{7,6},{8,9},{9,8},{10,11... | collective-permute-start | bytes 786440 | tf_op jit(solution)/shard_map/ppermute | solution.py:25
  4.1 20.4 %copy-start = (f32[512,1024]{1,0:T(8,128)S(1)}, f32[512,1024]{1,0:T(8,128)}, u32[]{:S(2)}) copy-start(f32[512,1024]{1,0:T(8,128)} %raw.1) | copy-start | bytes 6291460
  4.1 20.4 %copy-start.5 = (s32[4]{0:T(128)S(1)}, s32[4]{0:T(128)}, u32[]{:S(2)}) copy-start(s32[4]{0:T(128)} %starts.5) | copy-start | bytes 52
  4.1 20.4 %copy-start.6 = (s32[4]{0:T(128)S(1)}, s32[4]{0:T(128)}, u32[]{:S(2)}) copy-start(s32[4]{0:T(128)} %spans.5) | copy-start | bytes 52
  7.2 17.3 %collective-permute-start.2 = (f32[128,512]{1,0:T(8,128)S(1)}, f32[128,512]{1,0:T(8,128)S(1)}, u32[]{:S(2)}, u32[]{:S(2)}) collective-permute-start(f32[128,512]{1,0:T(8,128)S(1)} %get-tuple-element.20), channel_id=1, source_target_pairs={{2,0},{4,2},{6,4},{8,6},{10,8},{12,10},{14,12},{16,14},{18,16},{20... | collective-permute-start | bytes 786440 | tf_op jit(solution)/shard_map/ppermute | solution.py:20
  8.5 23.0 %collective-permute-start.4 = (f32[160,512]{1,0:T(8,128)S(1)}, f32[160,512]{1,0:T(8,128)S(1)}, u32[]{:S(2)}, u32[]{:S(2)}) collective-permute-start(f32[160,512]{1,0:T(8,128)S(1)} %get-tuple-element.27), channel_id=1, source_target_pairs={{2,0},{4,2},{6,4},{8,6},{10,8},{12,10},{14,12},{16,14},{18,16},{20... | collective-permute-start | bytes 983048 | tf_op jit(solution)/shard_map/ppermute | solution.py:20
  26.7 17.1 %collective-permute-start.6 = (f32[128,1024]{1,0:T(8,128)S(1)}, f32[128,1024]{1,0:T(8,128)S(1)}, u32[]{:S(2)}, u32[]{:S(2)}) collective-permute-start(f32[128,1024]{1,0:T(8,128)S(1)} %get-tuple-element.24.below), channel_id=1, source_target_pairs={{0,2},{2,4},{4,6},{6,8},{8,10},{10,12},{12,14},{14,16},{16,18},{18... | collective-permute-start | bytes 1572872 | tf_op jit(solution)/shard_map/ppermute | solution.py:20
  33.1 16.2 %collective-permute-start.7 = (f32[128,512]{1,0:T(8,128)S(1)}, f32[128,512]{1,0:T(8,128)S(1)}, u32[]{:S(2)}, u32[]{:S(2)}) collective-permute-start(f32[128,512]{1,0:T(8,128)S(1)} %get-tuple-element.33), channel_id=1, source_target_pairs={{0,2},{2,4},{4,6},{6,8},{8,10},{10,12},{12,14},{14,16},{16,18},{18... | collective-permute-start | bytes 786440 | tf_op jit(solution)/shard_map/ppermute | solution.py:20
  37.5 17.4 %collective-permute-start.5 = (f32[128,512]{1,0:T(8,128)S(1)}, f32[128,512]{1,0:T(8,128)S(1)}, u32[]{:S(2)}, u32[]{:S(2)}) collective-permute-start(f32[128,512]{1,0:T(8,128)S(1)} %get-tuple-element.28), channel_id=1, source_target_pairs={{0,2},{2,4},{4,6},{6,8},{8,10},{10,12},{12,14},{14,16},{16,18},{18... | collective-permute-start | bytes 786440 | tf_op jit(solution)/shard_map/ppermute | solution.py:20

commit v3 on v2

--- a/solution.py
+++ b/solution.py
@@ -10,7 +10,7 @@
 F32 = jnp.float32
 TILES = 2
 EIGHTHS_UP = (4, 4)
-EIGHTHS_DOWN = (4, 4)
+EIGHTHS_DOWN = (6, 2)
 VMEM_LIMIT = 24 * 1024 * 1024
 
 
@@ -53,6 +53,17 @@
 
 def stacked(upper, lower):
     return jnp.concatenate([upper, lower], axis=0)
+
+
+def unpacked(rows, width):
+    return jnp.concatenate(
+        [rows[:, at : at + width] for at in range(0, rows.shape[1], width)], axis=0
+    )
+
+
+def ordered(mine, other):
+    core = lax.axis_index("col")
+    return stacked(jnp.where(core == 0, mine, other), jnp.where(core == 0, other, mine))
 
 
 def is_active(starts, spans, step):
@@ -87,9 +98,10 @@
         early[step] = change_of(vectors[step], other[step], factors[step], core)
     last = messages[-1]
     extra = last.shape[0] - width
+    half = jnp.where(core == 0, early[1, : width // 2, :width], early[1, width // 2 : width, :width])
     for block in range(last.shape[1] // width):
-        last[width:, block * width : (block + 1) * width] = early[
-            1, block * extra : (block + 1) * extra, :width
+        last[width:, block * width : (block + 1) * width] = half[
+            block * extra : (block + 1) * extra
         ]
     for at, part in enumerate(parts):
         copies[2 + at].wait()
@@ -116,19 +128,12 @@
     cd[...] = jnp.where(is_active(starts, spans, 1), band - dot(border[1], band), band)
 
 
-def third_kernel(starts, spans, below, cd, border, *rest):
+def third_kernel(starts, spans, below, cd, border, half, *rest):
     count = len(EIGHTHS_UP)
     messages, d_out, sent = rest[:count], rest[count], rest[count + 1 :]
     width, cols = d_out.shape
     cuts = pieces(cols, EIGHTHS_DOWN)
-    last = messages[-1]
-    mixing = jnp.concatenate(
-        [
-            last[width:, block * width : (block + 1) * width]
-            for block in range(last.shape[1] // width)
-        ],
-        axis=0,
-    )
+    mixing = ordered(unpacked(messages[-1][width:], width), unpacked(half[...], width))
     for message, part in zip(messages, pieces(cols, EIGHTHS_UP)):
         low = below[:, part]
         low = low - dot(mixing, low) - message[:width]
@@ -143,7 +148,8 @@
                 ]
 
 
-def fourth_kernel(starts, spans, raw, above, bc, cd, d, second, late, border, out, before, held, sems):
+def fourth_kernel(starts, spans, raw, above, bc, cd, d, second, late, border, out, *rest):
+    *before, held, sems = rest
     width, cols = raw.shape
     span = cols // TILES
     first = lax.axis_index("row") == 0
@@ -164,7 +170,11 @@
         copy.start()
         copies.append(copy)
         ab = stacked(jnp.where(first, ab[:width], 0.0), low[:width])
-        before[:, here] = ab - dot(late[1], ab)
+        ab = ab - dot(late[1], ab)
+        for cut, kept in zip(pieces(cols, EIGHTHS_DOWN), before):
+            a, b = max(cut.start, here.start), min(cut.stop, here.stop)
+            if a < b:
+                kept[:, a - cut.start : b - cut.start] = ab[:, a - here.start : b - here.start]
     for copy in copies:
         copy.wait()
 
@@ -174,8 +184,8 @@
     width = above.shape[0]
     top = above[...]
     change = dot(late[0], top)
-    held[:width] = before[:width, cut] + (top - change[:width])
-    held[width:] = before[width:, cut] - change[width:]
+    held[:width] = before[:width] + (top - change[:width])
+    held[width:] = before[width:] - change[width:]
     copy = pltpu.make_async_copy(held, out.at[pl.ds(0, 2 * width), cut], sem)
     copy.start()
     copy.wait()
@@ -222,7 +232,9 @@
     fac_i, fac_b = inner_factor[0], border_factor[0]
 
     below = from_behind(panel[:width], "row", -1)
-    other_i = other_core(own_i)
+    own_early, fac_early = own_i[:2], fac_i[:2]
+    other_early = other_core(own_early)
+    other_late = other_core(own_i[2:])
     other_b = other_core(own_b)
 
     square = (2 * width, 2 * width)
@@ -230,7 +242,7 @@
     ups = [part.stop - part.start for part in pieces(cols, EIGHTHS_UP)]
     cuts = pieces(cols, EIGHTHS_DOWN)
     downs = [cut.stop - cut.start for cut in cuts]
-    extra = width * width // ups[-1]
+    extra = width * width // (lax.axis_size("col") * ups[-1])
     shapes = [(width, up) for up in ups[:-1]] + [(width + extra, ups[-1])]
     early, bc, *up_messages = call(
         first_kernel,
@@ -238,7 +250,7 @@
         [hbm(), whole((2, width, width)), hbm(), hbm()],
         [whole((2,) + square), whole((2 * width, cols))] + [whole(shape) for shape in shapes],
         [(2,) + square, (2 * width, cols)] + shapes,
-        [own_i[:2], other_i, fac_i[:2], panel],
+        [own_early, other_early, fac_early, panel],
         "inner_and_up",
         vmem=50 * 1024 * 1024,
         scratch_shapes=[
@@ -253,10 +265,10 @@
     late, border = call(
         matrix_kernel,
         1,
-        [whole((2, width, width), (1, 0, 0))] * 3 + [whole(vec)] * 3,
+        [whole((2, width, width), (1, 0, 0)), whole((2, width, width)), whole((2, width, width), (1, 0, 0))] + [whole(vec)] * 3,
         [whole((2,) + square), whole((steps,) + square)],
         [(2,) + square, (steps,) + square],
-        [own_i, other_i, fac_i, own_b, other_b, fac_b],
+        [own_i, other_late, fac_i, own_b, other_b, fac_b],
         "matrices",
     )
     down_message, cd = call(
@@ -272,31 +284,31 @@
     d, *sent = call(
         third_kernel,
         1,
-        [smem(), smem(), whole((width, cols)), whole((2 * width, cols)), whole((1,) + square, (2, 0, 0))] + [whole(shape) for shape in shapes],
+        [smem(), smem(), whole((width, cols)), whole((2 * width, cols)), whole((1,) + square, (2, 0, 0)), whole((extra, ups[-1]))] + [whole(shape) for shape in shapes],
         [whole((width, cols))] + [whole((width, down)) for down in downs],
         [(width, cols)] + [(width, down) for down in downs],
-        [group_start, group_span, down_message, cd, border] + from_below,
+        [group_start, group_span, down_message, cd, border, other_core(from_below[-1][width:])] + from_below,
         "second_border",
     )
     last = [from_behind(part, "row", 1) for part in sent]
-    out, before = call(
+    out, *before = call(
         fourth_kernel,
         1,
         [smem(), smem(), whole((width, cols)), whole((width, cols)), whole((2 * width, cols)), whole((2 * width, cols)), whole((width, cols)), whole((1,) + square, (1, 0, 0)), whole((2,) + square), whole((1,) + square, (3, 0, 0))],
-        [pl.BlockSpec(memory_space=pl.ANY), whole((2 * width, cols))],
-        [(height, cols), (2 * width, cols)],
+        [pl.BlockSpec(memory_space=pl.ANY)] + [whole((2 * width, down)) for down in downs],
+        [(height, cols)] + [(2 * width, down) for down in downs],
         [group_start, group_span, panel, above, bc, cd, d, early, late, border],
         "rest",
         scratch_shapes=[pltpu.VMEM((2 * width, cols), F32), pltpu.SemaphoreType.DMA((TILES,))],
     )
-    for cut, down, part in zip(cuts, downs, last):
+    for cut, down, part, kept in zip(cuts, downs, last, before):
         (out,) = call(
             functools.partial(last_kernel, cut),
             1,
-            [whole((width, down)), whole((1, 2 * width, width), (1, 0, 0)), whole((2 * width, cols)), pl.BlockSpec(memory_space=pl.ANY)],
+            [whole((width, down)), whole((1, 2 * width, width), (1, 0, 0)), whole((2 * width, down)), pl.BlockSpec(memory_space=pl.ANY)],
             [pl.BlockSpec(memory_space=pl.ANY)],
             [(height, cols)],
-            [part, late, before, out],
+            [part, late, kept, out],
             "finish",
             scratch_shapes=[pltpu.VMEM((2 * width, down), F32), pltpu.SemaphoreType.DMA],
             input_output_aliases={3: 0},

time: 56.3 us -> 54.8 us (0.973)
  waiting for transfers between devices: 22.4 us -> 19.3 us
  local copies, waits for them, and re-layouts: 2.09 us -> 3.23 us
  starting transfers between devices: 17 us -> 17.7 us
    ppermute x6, waiting for transfers between devices: 22.4 us -> 17.1 us  [from_behind(): return lax.ppermute(value, axis, pairs)]
    ppermute x2 -> x4, waiting for transfers between devices: 0.01 us -> 2.19 us  [other_core(): lax.ppermute(value, 'col', [(i, (i + 1) % cores) for i in range(cores)])]
    slice x1 -> x3, local copies, waits for them, and re-layouts: 0.99 us -> 2.04 us  [the longest x1 1.04 us: local(): own_early, fac_early = (own_i[:2], fac_i[:2])]
    ppermute x2 -> x4, starting transfers between devices: 0.7 us -> 1.24 us  [other_core(): lax.ppermute(value, 'col', [(i, (i + 1) % cores) for i in range(cores)])]
  transfers between devices with their start and end apart: 8 -> 10, of which waited for: 5 -> 5; matrix products, arithmetic and copies ran while one was open for 4% -> 4% of each run, Pallas kernels for 23% -> 24%
where the time goes in v3:
time: 54.8 us; the launch traced here: 54.4 us
  waiting for transfers between devices  19.3 us (35%)
  starting transfers between devices  17.7 us (32%)
  Pallas kernels  14.1 us (26%)
  local copies, waits for them, and re-layouts  3.23 us (6%)
    ppermute x6, waiting for transfers between devices, from_behind(): return lax.ppermute(value, axis, pairs)  17.1 us
    ppermute x6, starting transfers between devices, from_behind(): return lax.ppermute(value, axis, pairs)  16.4 us
    pallas_call x7, Pallas kernels, call(): pl.pallas_call(kernel, grid=(tiles,), in_specs=in_specs, out_specs=out_sp...  14.1 us
    ppermute x4, waiting for transfers between devices, other_core(): lax.ppermute(value, 'col', [(i, (i + 1) % cores) for i in range(cores)])  2.19 us
    ppermute x4, starting transfers between devices, other_core(): lax.ppermute(value, 'col', [(i, (i + 1) % cores) for i in range(cores)])  1.24 us
    slice x1, local copies, waits for them, and re-layouts, local(): below = from_behind(panel[:width], 'row', -1)  1.17 us
  transfers between devices with their start and end apart: 10, of which 5 were waited for; matrix products, arithmetic and copies ran while one was open for 4% of the time, Pallas kernels for 24%

profile of v3, /device:TPU:0, one launch (start us, length us, event | category | flops | bytes accessed | tf_op | source)
XLA Modules:
  0.0 54.4 jit_solution(16069684824886944073)
XLA Ops:
  0.0 0.0 copy-start.1
  0.0 0.0 copy-start.3
  0.0 0.0 copy-start.2
  0.0 0.0 copy-start.4
  0.0 1.2 %slice.24 = f32[128,1024]{1,0:T(8,128)S(1)} slice(f32[512,1024]{1,0:T(8,128)} %raw.1), slice={[0:128], [0:1024]} | slice | bytes 1048576 | tf_op jit(solution)/shard_map/slice | solution.py:234
  1.2 1.3 %collective-permute-start = (f32[128,1024]{1,0:T(8,128)S(1)}, f32[128,1024]{1,0:T(8,128)S(1)}, u32[]{:S(2)}, u32[]{:S(2)}) collective-permute-start(f32[128,1024]{1,0:T(8,128)S(1)} %slice.24), channel_id=1, source_target_pairs={{2,0},{4,2},{6,4},{8,6},{10,8},{12,10},{14,12},{16,14},{18,16},{20... | collective-permute-start | bytes 1572872 | tf_op jit(solution)/shard_map/ppermute | solution.py:20
  2.5 1.0 %slice_bitcast_fusion = (f32[2,128,128]{2,1,0:T(8,128)S(1)}, f32[2,128,128]{2,1,0:T(8,128)S(1)}) fusion(f32[1,4,128,128]{3,2,1,0:T(8,128)} %param.8), kind=kLoop, calls=%fused_computation | loop fusion | bytes 524288 | tf_op jit(solution)/shard_map/slice | solution.py:237
  3.5 0.5 collective-permute-start.1
  4.0 0.0 copy-start
  4.0 0.0 copy-start.5
  4.0 0.0 copy-start.6
  4.0 0.1 collective-permute-start.4
  4.1 1.0 %slice_bitcast_fusion.1.factor = f32[2,128,128]{2,1,0:T(8,128)S(1)} fusion(f32[1,4,128,128]{3,2,1,0:T(8,128)} %param.9), kind=kLoop, calls=%fused_computation.1 | loop fusion | bytes 262144 | tf_op jit(solution)/shard_map/slice | solution.py:235
  5.2 0.0 collective-permute-done.1.other
  5.2 2.8 %inner_and_up.1 = (f32[2,256,256]{2,1,0:T(8,128)S(1)}, f32[256,1024]{1,0:T(8,128)S(1)}, f32[128,512]{1,0:T(8,128)S(1)}, f32[144,512]{1,0:T(8,128)S(1)}) custom-call(f32[2,128,128]{2,1,0:T(8,128)S(1)} %get-tuple-element.38.own, f32[2,128,128]{2,1,0:T(8,128)S(1)} %collective-permute-done.1.other, f32[2,128,128]{2,1,0:T(8,128)S(1)} %slice_bitcast_fusion.1.factor, ...), custom_call_target="tpu_custom_call" | custom-call | flops 1 | bytes 1 | tf_op jit(solution)/shard_map/inner_and_up/pallas_call | solution.py:213
  8.0 1.3 %collective-permute-start.2 = (f32[128,512]{1,0:T(8,128)S(1)}, f32[128,512]{1,0:T(8,128)S(1)}, u32[]{:S(2)}, u32[]{:S(2)}) collective-permute-start(f32[128,512]{1,0:T(8,128)S(1)} %get-tuple-element.21), channel_id=1, source_target_pairs={{2,0},{4,2},{6,4},{8,6},{10,8},{12,10},{14,12},{16,14},{18,16},{20... | collective-permute-start | bytes 786440 | tf_op jit(solution)/shard_map/ppermute | solution.py:20
  9.3 1.3 %collective-permute-start.5 = (f32[144,512]{1,0:T(8,128)S(1)}, f32[144,512]{1,0:T(8,128)S(1)}, u32[]{:S(2)}, u32[]{:S(2)}) collective-permute-start(f32[144,512]{1,0:T(8,128)S(1)} %get-tuple-element.27), channel_id=1, source_target_pairs={{2,0},{4,2},{6,4},{8,6},{10,8},{12,10},{14,12},{16,14},{18,16},{20... | collective-permute-start | bytes 884744 | tf_op jit(solution)/shard_map/ppermute | solution.py:20
  10.6 0.5 collective-permute-start.3
  11.2 1.0 %collective-permute-done.3.other_i = f32[2,128,128]{2,1,0:T(8,128)S(1)} collective-permute-done((f32[2,128,128]{2,1,0:T(8,128)S(1)}, f32[2,128,128]{2,1,0:T(8,128)S(1)}, u32[]{:S(2)}, u32[]{:S(2)}) %collective-permute-start.3) | collective-permute-done | bytes 131104 | tf_op jit(solution)/shard_map/ppermute | solution.py:25
  12.1 0.0 collective-permute-done.4.other_b
  12.2 0.0 copy-done.1
  12.2 0.0 copy-done.3
  12.2 0.0 copy-done.2
  12.2 0.0 copy-done.4
  12.2 1.4 %matrices.1 = (f32[2,256,256]{2,1,0:T(8,128)S(1)}, f32[4,256,256]{2,1,0:T(8,128)S(1)}) custom-call(f32[4,128,128]{2,1,0:T(8,128)S(1)} %bitcast.10, f32[2,128,128]{2,1,0:T(8,128)S(1)} %collective-permute-done.3.other_i, f32[4,128,128]{2,1,0:T(8,128)S(1)} %bitcast.11, f32[4,128,128]{2,1,0:T(8,128)S(1)} %bitcast.13, ...), custom_call_target="tpu_custom_call" | custom-call | flops 1 | bytes 1 | tf_op jit(solution)/shard_map/matrices/pallas_call | solution.py:213
  13.6 10.9 %collective-permute-done.2.rest_0_ = f32[128,512]{1,0:T(8,128)S(1)} collective-permute-done((f32[128,512]{1,0:T(8,128)S(1)}, f32[128,512]{1,0:T(8,128)S(1)}, u32[]{:S(2)}, u32[]{:S(2)}) %collective-permute-start.2) | collective-permute-done | bytes 262176 | tf_op jit(solution)/shard_map/ppermute | solution.py:20
  24.4 0.0 collective-permute-done.below
  24.4 0.0 copy-done
  24.4 0.0 copy-done.5
  24.4 0.0 copy-done.6
  24.4 2.2 %border_and_down.1 = (f32[128,1024]{1,0:T(8,128)S(1)}, f32[256,1024]{1,0:T(8,128)S(1)}) custom-call(s32[4]{0:T(128)S(1)} %copy-done.5, s32[4]{0:T(128)S(1)} %copy-done.6, f32[512,1024]{1,0:T(8,128)S(1)} %copy-done, f32[128,1024]{1,0:T(8,128)S(1)} %collective-permute-done.below, f32[256,1024]{1,0:T(8,128)S(1)} %get-tuple-element.23.c.bc, ...), custom_call_target="tpu_custom_call" | custom-call | flops 1 | bytes 1 | tf_op jit(solution)/shard_map/border_and_down/pallas_call | solution.py:213
  26.6 4.9 %collective-permute-start.8 = (f32[128,1024]{1,0:T(8,128)S(1)}, f32[128,1024]{1,0:T(8,128)S(1)}, u32[]{:S(2)}, u32[]{:S(2)}) collective-permute-start(f32[128,1024]{1,0:T(8,128)S(1)} %get-tuple-element.25.below), channel_id=1, source_target_pairs={{0,2},{2,4},{4,6},{6,8},{8,10},{10,12},{12,14},{14,16},{16,18},{18... | collective-permute-start | bytes 1572872 | tf_op jit(solution)/shard_map/ppermute | solution.py:20
  31.5 0.0 collective-permute-done.5.rest_1_
  31.5 0.1 collective-permute-start.6
  31.6 1.2 %collective-permute-done.6.half = f32[16,512]{1,0:T(8,128)S(1)} collective-permute-done((f32[16,512]{1,0:T(8,128)S(1)}, f32[16,512]{1,0:T(8,128)S(1)}, u32[]{:S(2)}, u32[]{:S(2)}) %collective-permute-start.6) | collective-permute-done | bytes 32800 | tf_op jit(solution)/shard_map/ppermute | solution.py:25
  32.8 1.6 %second_border.1 = (f32[128,1024]{1,0:T(8,128)S(1)}, f32[128,768]{1,0:T(8,128)S(1)}, f32[128,256]{1,0:T(8,128)S(1)}) custom-call(s32[4]{0:T(128)S(1)} %copy-done.5, s32[4]{0:T(128)S(1)} %copy-done.6, f32[128,1024]{1,0:T(8,128)S(1)} %get-tuple-element.25.below, f32[256,1024]{1,0:T(8,128)S(1)} %get-tuple-element.26.cd, ...), custom_call_target="tpu_custom_call" | custom-call | flops 1 | bytes 1 | tf_op jit(solution)/shard_map/second_border/pallas_call | solution.py:213
  34.5 2.9 %collective-permute-start.9 = (f32[128,768]{1,0:T(8,128)S(1)}, f32[128,768]{1,0:T(8,128)S(1)}, u32[]{:S(2)}, u32[]{:S(2)}) collective-permute-start(f32[128,768]{1,0:T(8,128)S(1)} %get-tuple-element.34), channel_id=1, source_target_pairs={{0,2},{2,4},{4,6},{6,8},{8,10},{10,12},{12,14},{14,16},{16,18},{18... | collective-permute-start | bytes 1179656 | tf_op jit(solution)/shard_map/ppermute | solution.py:20
  37.3 4.8 %collective-permute-start.7 = (f32[128,256]{1,0:T(8,128)S(1)}, f32[128,256]{1,0:T(8,128)S(1)}, u32[]{:S(2)}, u32[]{:S(2)}) collective-permute-start(f32[128,256]{1,0:T(8,128)S(1)} %get-tuple-element.29), channel_id=1, source_target_pairs={{0,2},{2,4},{4,6},{6,8},{8,10},{10,12},{12,14},{14,16},{16,18},{18... | collective-permute-start | bytes 393224 | tf_op jit(solution)/shard_map/ppermute | solution.py:20
  42.1 1.7 %collective-permute-done.8.above = f32[128,1024]{1,0:T(8,128)S(1)} collective-permute-done((f32[128,1024]{1,0:T(8,128)S(1)}, f32[128,1024]{1,0:T(8,128)S(1)}, u32[]{:S(2)}, u32[]{:S(2)}) %collective-permute-start.8) | collective-permute-done | bytes 524320 | tf_op jit(solution)/shard_map/ppermute | solution.py:20
  43.9 3.7 %rest.1 = (f32[512,1024]{1,0:T(8,128)}, f32[256,768]{1,0:T(8,128)S(1)}, f32[256,256]{1,0:T(8,128)S(1)}) custom-call(s32[4]{0:T(128)S(1)} %copy-done.5, s32[4]{0:T(128)S(1)} %copy-done.6, f32[512,1024]{1,0:T(8,128)S(1)} %copy-done, f32[128,1024]{1,0:T(8,128)S(1)} %collective-permute-done.8.above, f32[256,1024]{1,0:T(8,128)S(1)} %get-tuple-element.23.c.bc, ...), custom_call_target="tpu_custom_call" | custom-call | flops 1 | bytes 1 | tf_op jit(solution)/shard_map/rest/pallas_call | solution.py:213
  47.6 4.5 %collective-permute-done.9.above = f32[128,768]{1,0:T(8,128)S(1)} collective-permute-done((f32[128,768]{1,0:T(8,128)S(1)}, f32[128,768]{1,0:T(8,128)S(1)}, u32[]{:S(2)}, u32[]{:S(2)}) %collective-permute-start.9) | collective-permute-done | bytes 393248 | tf_op jit(solution)/shard_map/ppermute | solution.py:20
  52.1 1.4 %finish.2.out_in = f32[512,1024]{1,0:T(8,128)} custom-call(f32[128,768]{1,0:T(8,128)S(1)} %collective-permute-done.9.above, f32[2,256,256]{2,1,0:T(8,128)S(1)} %get-tuple-element.30.late, f32[256,768]{1,0:T(8,128)S(1)} %get-tuple-element.35.before, f32[512,1024]{1,0:T(8,128)} %get-tuple-element.36.out_in), custom_call_target="tpu_custom_call", output_to_operand_aliasing={{}: (3, {})} | custom-call | flops 1 | bytes 1 | tf_op jit(solution)/shard_map/finish/pallas_call | solution.py:213
  53.4 0.0 collective-permute-done.7.above
  53.5 1.0 %finish.3 = f32[512,1024]{1,0:T(8,128)} custom-call(f32[128,256]{1,0:T(8,128)S(1)} %collective-permute-done.7.above, f32[2,256,256]{2,1,0:T(8,128)S(1)} %get-tuple-element.30.late, f32[256,256]{1,0:T(8,128)S(1)} %get-tuple-element.33.before, f32[512,1024]{1,0:T(8,128)} %finish.2.out_in), custom_call_target="tpu_custom_call", output_to_operand_aliasing={{}: (3, {})} | custom-call | flops 1 | bytes 1 | tf_op jit(solution)/shard_map/finish/pallas_call | solution.py:213
  (1 shorter events, 0.0 us)
Async XLA Ops:
  0.0 12.2 %copy-start.1 = (f32[1,4,128,128]{3,2,1,0:T(8,128)S(1)}, f32[1,4,128,128]{3,2,1,0:T(8,128)}, u32[]{:S(2)}) copy-start(f32[1,4,128,128]{3,2,1,0:T(8,128)} %param.8) | copy-start | bytes 786436
  0.0 12.2 %copy-start.3 = (f32[1,4,128,128]{3,2,1,0:T(8,128)S(1)}, f32[1,4,128,128]{3,2,1,0:T(8,128)}, u32[]{:S(2)}) copy-start(f32[1,4,128,128]{3,2,1,0:T(8,128)} %param.10) | copy-start | bytes 786436
  0.0 12.2 %copy-start.2 = (f32[1,4,128,128]{3,2,1,0:T(8,128)S(1)}, f32[1,4,128,128]{3,2,1,0:T(8,128)}, u32[]{:S(2)}) copy-start(f32[1,4,128,128]{3,2,1,0:T(8,128)} %param.9) | copy-start | bytes 786436
  0.0 12.2 %copy-start.4 = (f32[1,4,128,128]{3,2,1,0:T(8,128)S(1)}, f32[1,4,128,128]{3,2,1,0:T(8,128)}, u32[]{:S(2)}) copy-start(f32[1,4,128,128]{3,2,1,0:T(8,128)} %param.11) | copy-start | bytes 786436
  1.2 23.2 %collective-permute-start = (f32[128,1024]{1,0:T(8,128)S(1)}, f32[128,1024]{1,0:T(8,128)S(1)}, u32[]{:S(2)}, u32[]{:S(2)}) collective-permute-start(f32[128,1024]{1,0:T(8,128)S(1)} %slice.24), channel_id=1, source_target_pairs={{2,0},{4,2},{6,4},{8,6},{10,8},{12,10},{14,12},{16,14},{18,16},{20... | collective-permute-start | bytes 1572872 | tf_op jit(solution)/shard_map/ppermute | solution.py:20
  3.5 1.7 %collective-permute-start.1 = (f32[2,128,128]{2,1,0:T(8,128)S(1)}, f32[2,128,128]{2,1,0:T(8,128)S(1)}, u32[]{:S(2)}, u32[]{:S(2)}) collective-permute-start(f32[2,128,128]{2,1,0:T(8,128)S(1)} %get-tuple-element.38.own), channel_id=1, source_target_pairs={{0,1},{1,0},{2,3},{3,2},{4,5},{5,4},{6,7},{7,6},{8,9},{9,8},{10,11... | collective-permute-start | bytes 393224 | tf_op jit(solution)/shard_map/ppermute | solution.py:25
  4.0 20.4 %copy-start = (f32[512,1024]{1,0:T(8,128)S(1)}, f32[512,1024]{1,0:T(8,128)}, u32[]{:S(2)}) copy-start(f32[512,1024]{1,0:T(8,128)} %raw.1) | copy-start | bytes 6291460
  4.0 20.4 %copy-start.5 = (s32[4]{0:T(128)S(1)}, s32[4]{0:T(128)}, u32[]{:S(2)}) copy-start(s32[4]{0:T(128)} %starts.5) | copy-start | bytes 52
  4.0 20.4 %copy-start.6 = (s32[4]{0:T(128)S(1)}, s32[4]{0:T(128)}, u32[]{:S(2)}) copy-start(s32[4]{0:T(128)} %spans.5) | copy-start | bytes 52
  4.0 8.1 %collective-permute-start.4 = (f32[4,128,128]{2,1,0:T(8,128)}, f32[4,128,128]{2,1,0:T(8,128)S(1)}, u32[]{:S(2)}, u32[]{:S(2)}) collective-permute-start(f32[4,128,128]{2,1,0:T(8,128)} %bitcast.12), channel_id=1, source_target_pairs={{0,1},{1,0},{2,3},{3,2},{4,5},{5,4},{6,7},{7,6},{8,9},{9,8},{10,11... | collective-permute-start | bytes 786440 | tf_op jit(solution)/shard_map/ppermute | solution.py:25
  8.0 16.4 %collective-permute-start.2 = (f32[128,512]{1,0:T(8,128)S(1)}, f32[128,512]{1,0:T(8,128)S(1)}, u32[]{:S(2)}, u32[]{:S(2)}) collective-permute-start(f32[128,512]{1,0:T(8,128)S(1)} %get-tuple-element.21), channel_id=1, source_target_pairs={{2,0},{4,2},{6,4},{8,6},{10,8},{12,10},{14,12},{16,14},{18,16},{20... | collective-permute-start | bytes 786440 | tf_op jit(solution)/shard_map/ppermute | solution.py:20
  9.3 22.2 %collective-permute-start.5 = (f32[144,512]{1,0:T(8,128)S(1)}, f32[144,512]{1,0:T(8,128)S(1)}, u32[]{:S(2)}, u32[]{:S(2)}) collective-permute-start(f32[144,512]{1,0:T(8,128)S(1)} %get-tuple-element.27), channel_id=1, source_target_pairs={{2,0},{4,2},{6,4},{8,6},{10,8},{12,10},{14,12},{16,14},{18,16},{20... | collective-permute-start | bytes 884744 | tf_op jit(solution)/shard_map/ppermute | solution.py:20
  10.6 1.5 %collective-permute-start.3 = (f32[2,128,128]{2,1,0:T(8,128)S(1)}, f32[2,128,128]{2,1,0:T(8,128)S(1)}, u32[]{:S(2)}, u32[]{:S(2)}) collective-permute-start(f32[2,128,128]{2,1,0:T(8,128)S(1)} %get-tuple-element.37), channel_id=1, source_target_pairs={{0,1},{1,0},{2,3},{3,2},{4,5},{5,4},{6,7},{7,6},{8,9},{9,8},{10,11... | collective-permute-start | bytes 393224 | tf_op jit(solution)/shard_map/ppermute | solution.py:25
  26.6 17.2 %collective-permute-start.8 = (f32[128,1024]{1,0:T(8,128)S(1)}, f32[128,1024]{1,0:T(8,128)S(1)}, u32[]{:S(2)}, u32[]{:S(2)}) collective-permute-start(f32[128,1024]{1,0:T(8,128)S(1)} %get-tuple-element.25.below), channel_id=1, source_target_pairs={{0,2},{2,4},{4,6},{6,8},{8,10},{10,12},{12,14},{14,16},{16,18},{18... | collective-permute-start | bytes 1572872 | tf_op jit(solution)/shard_map/ppermute | solution.py:20
  31.5 1.3 %collective-permute-start.6 = (f32[16,512]{1,0:T(8,128)S(1)}, f32[16,512]{1,0:T(8,128)S(1)}, u32[]{:S(2)}, u32[]{:S(2)}) collective-permute-start(f32[16,512]{1,0:T(8,128)S(1)} %slice.32), channel_id=1, source_target_pairs={{0,1},{1,0},{2,3},{3,2},{4,5},{5,4},{6,7},{7,6},{8,9},{9,8},{10,11... | collective-permute-start | bytes 98312 | tf_op jit(solution)/shard_map/ppermute | solution.py:25
  34.5 17.6 %collective-permute-start.9 = (f32[128,768]{1,0:T(8,128)S(1)}, f32[128,768]{1,0:T(8,128)S(1)}, u32[]{:S(2)}, u32[]{:S(2)}) collective-permute-start(f32[128,768]{1,0:T(8,128)S(1)} %get-tuple-element.34), channel_id=1, source_target_pairs={{0,2},{2,4},{4,6},{6,8},{8,10},{10,12},{12,14},{14,16},{16,18},{18... | collective-permute-start | bytes 1179656 | tf_op jit(solution)/shard_map/ppermute | solution.py:20
  37.3 16.2 %collective-permute-start.7 = (f32[128,256]{1,0:T(8,128)S(1)}, f32[128,256]{1,0:T(8,128)S(1)}, u32[]{:S(2)}, u32[]{:S(2)}) collective-permute-start(f32[128,256]{1,0:T(8,128)S(1)} %get-tuple-element.29), channel_id=1, source_target_pairs={{0,2},{2,4},{4,6},{6,8},{8,10},{10,12},{12,14},{14,16},{16,18},{18... | collective-permute-start | bytes 393224 | tf_op jit(solution)/shard_map/ppermute | solution.py:20

commit v4 on v3

--- a/solution.py
+++ b/solution.py
@@ -42,6 +42,10 @@
     xh, xl = split(x)
     yh, yl = split(y)
     return product(xl, yh) + product(xh, yl) + product(xh, yh)
+
+
+def exact_dot(x, y):
+    return jnp.dot(x, y, precision=lax.Precision.HIGHEST, preferred_element_type=F32)
 
 
 def change_of(first, second, factor, core):
@@ -125,7 +129,7 @@
     band = jnp.where(is_active(starts, spans, 0), band - dot(border[0], band), band)
     message[...] = band[width:]
     band = stacked(c[...], band[:width])
-    cd[...] = jnp.where(is_active(starts, spans, 1), band - dot(border[1], band), band)
+    cd[...] = jnp.where(is_active(starts, spans, 1), band - exact_dot(border[1], band), band)
 
 
 def third_kernel(starts, spans, below, cd, border, half, *rest):

time: 54.8 us -> 54.8 us (level)
  transfers between devices with their start and end apart: 10 -> 10, of which waited for: 5 -> 5; matrix products, arithmetic and copies ran while one was open for 4% -> 4% of each run, Pallas kernels for 24% -> 25%
where the time goes in v4:
time: 54.8 us; the launch traced here: 54.4 us
  waiting for transfers between devices  18.8 us (34%)
  starting transfers between devices  17.7 us (32%)
  Pallas kernels  14.6 us (27%)
  local copies, waits for them, and re-layouts  3.23 us (6%)
    ppermute x6, waiting for transfers between devices, from_behind(): return lax.ppermute(value, axis, pairs)  16.6 us
    ppermute x6, starting transfers between devices, from_behind(): return lax.ppermute(value, axis, pairs)  16.4 us
    pallas_call x7, Pallas kernels, call(): pl.pallas_call(kernel, grid=(tiles,), in_specs=in_specs, out_specs=out_sp...  14.6 us
    ppermute x4, waiting for transfers between devices, other_core(): lax.ppermute(value, 'col', [(i, (i + 1) % cores) for i in range(cores)])  2.19 us
    ppermute x4, starting transfers between devices, other_core(): lax.ppermute(value, 'col', [(i, (i + 1) % cores) for i in range(cores)])  1.24 us
    slice x1, local copies, waits for them, and re-layouts, local(): below = from_behind(panel[:width], 'row', -1)  1.17 us
  transfers between devices with their start and end apart: 10, of which 5 were waited for; matrix products, arithmetic and copies ran while one was open for 4% of the time, Pallas kernels for 25%

profile of v4, /device:TPU:0, one launch (start us, length us, event | category | flops | bytes accessed | tf_op | source)
XLA Modules:
  0.0 54.4 jit_solution(16553231229843348523)
XLA Ops:
  0.0 0.0 copy-start.1
  0.0 0.0 copy-start.3
  0.0 0.0 copy-start.2
  0.0 0.0 copy-start.4
  0.0 1.2 %slice.24 = f32[128,1024]{1,0:T(8,128)S(1)} slice(f32[512,1024]{1,0:T(8,128)} %raw.1), slice={[0:128], [0:1024]} | slice | bytes 1048576 | tf_op jit(solution)/shard_map/slice | solution.py:238
  1.2 1.3 %collective-permute-start = (f32[128,1024]{1,0:T(8,128)S(1)}, f32[128,1024]{1,0:T(8,128)S(1)}, u32[]{:S(2)}, u32[]{:S(2)}) collective-permute-start(f32[128,1024]{1,0:T(8,128)S(1)} %slice.24), channel_id=1, source_target_pairs={{2,0},{4,2},{6,4},{8,6},{10,8},{12,10},{14,12},{16,14},{18,16},{20... | collective-permute-start | bytes 1572872 | tf_op jit(solution)/shard_map/ppermute | solution.py:20
  2.5 1.0 %slice_bitcast_fusion = (f32[2,128,128]{2,1,0:T(8,128)S(1)}, f32[2,128,128]{2,1,0:T(8,128)S(1)}) fusion(f32[1,4,128,128]{3,2,1,0:T(8,128)} %param.8), kind=kLoop, calls=%fused_computation | loop fusion | bytes 524288 | tf_op jit(solution)/shard_map/slice | solution.py:241
  3.5 0.5 collective-permute-start.1
  4.0 0.0 copy-start
  4.0 0.0 copy-start.5
  4.0 0.0 copy-start.6
  4.0 0.1 collective-permute-start.4
  4.1 1.0 %slice_bitcast_fusion.1.factor = f32[2,128,128]{2,1,0:T(8,128)S(1)} fusion(f32[1,4,128,128]{3,2,1,0:T(8,128)} %param.9), kind=kLoop, calls=%fused_computation.1 | loop fusion | bytes 262144 | tf_op jit(solution)/shard_map/slice | solution.py:239
  5.2 0.0 collective-permute-done.1.other
  5.2 2.8 %inner_and_up.1 = (f32[2,256,256]{2,1,0:T(8,128)S(1)}, f32[256,1024]{1,0:T(8,128)S(1)}, f32[128,512]{1,0:T(8,128)S(1)}, f32[144,512]{1,0:T(8,128)S(1)}) custom-call(f32[2,128,128]{2,1,0:T(8,128)S(1)} %get-tuple-element.38.own, f32[2,128,128]{2,1,0:T(8,128)S(1)} %collective-permute-done.1.other, f32[2,128,128]{2,1,0:T(8,128)S(1)} %slice_bitcast_fusion.1.factor, ...), custom_call_target="tpu_custom_call" | custom-call | flops 1 | bytes 1 | tf_op jit(solution)/shard_map/inner_and_up/pallas_call | solution.py:217
  8.0 1.3 %collective-permute-start.2 = (f32[128,512]{1,0:T(8,128)S(1)}, f32[128,512]{1,0:T(8,128)S(1)}, u32[]{:S(2)}, u32[]{:S(2)}) collective-permute-start(f32[128,512]{1,0:T(8,128)S(1)} %get-tuple-element.21), channel_id=1, source_target_pairs={{2,0},{4,2},{6,4},{8,6},{10,8},{12,10},{14,12},{16,14},{18,16},{20... | collective-permute-start | bytes 786440 | tf_op jit(solution)/shard_map/ppermute | solution.py:20
  9.3 1.3 %collective-permute-start.5 = (f32[144,512]{1,0:T(8,128)S(1)}, f32[144,512]{1,0:T(8,128)S(1)}, u32[]{:S(2)}, u32[]{:S(2)}) collective-permute-start(f32[144,512]{1,0:T(8,128)S(1)} %get-tuple-element.27), channel_id=1, source_target_pairs={{2,0},{4,2},{6,4},{8,6},{10,8},{12,10},{14,12},{16,14},{18,16},{20... | collective-permute-start | bytes 884744 | tf_op jit(solution)/shard_map/ppermute | solution.py:20
  10.6 0.5 collective-permute-start.3
  11.2 1.0 %collective-permute-done.3.other_i = f32[2,128,128]{2,1,0:T(8,128)S(1)} collective-permute-done((f32[2,128,128]{2,1,0:T(8,128)S(1)}, f32[2,128,128]{2,1,0:T(8,128)S(1)}, u32[]{:S(2)}, u32[]{:S(2)}) %collective-permute-start.3) | collective-permute-done | bytes 131104 | tf_op jit(solution)/shard_map/ppermute | solution.py:25
  12.1 0.0 collective-permute-done.4.other_b
  12.2 0.0 copy-done.1
  12.2 0.0 copy-done.3
  12.2 0.0 copy-done.2
  12.2 0.0 copy-done.4
  12.2 1.4 %matrices.1 = (f32[2,256,256]{2,1,0:T(8,128)S(1)}, f32[4,256,256]{2,1,0:T(8,128)S(1)}) custom-call(f32[4,128,128]{2,1,0:T(8,128)S(1)} %bitcast.10, f32[2,128,128]{2,1,0:T(8,128)S(1)} %collective-permute-done.3.other_i, f32[4,128,128]{2,1,0:T(8,128)S(1)} %bitcast.11, f32[4,128,128]{2,1,0:T(8,128)S(1)} %bitcast.13, ...), custom_call_target="tpu_custom_call" | custom-call | flops 1 | bytes 1 | tf_op jit(solution)/shard_map/matrices/pallas_call | solution.py:217
  13.6 10.9 %collective-permute-done.2.rest_0_ = f32[128,512]{1,0:T(8,128)S(1)} collective-permute-done((f32[128,512]{1,0:T(8,128)S(1)}, f32[128,512]{1,0:T(8,128)S(1)}, u32[]{:S(2)}, u32[]{:S(2)}) %collective-permute-start.2) | collective-permute-done | bytes 262176 | tf_op jit(solution)/shard_map/ppermute | solution.py:20
  24.4 0.0 collective-permute-done.below
  24.4 0.0 copy-done
  24.4 0.0 copy-done.5
  24.4 0.0 copy-done.6
  24.4 2.7 %border_and_down.1 = (f32[128,1024]{1,0:T(8,128)S(1)}, f32[256,1024]{1,0:T(8,128)S(1)}) custom-call(s32[4]{0:T(128)S(1)} %copy-done.5, s32[4]{0:T(128)S(1)} %copy-done.6, f32[512,1024]{1,0:T(8,128)S(1)} %copy-done, f32[128,1024]{1,0:T(8,128)S(1)} %collective-permute-done.below, f32[256,1024]{1,0:T(8,128)S(1)} %get-tuple-element.23.c.bc, ...), custom_call_target="tpu_custom_call" | custom-call | flops 1 | bytes 1 | tf_op jit(solution)/shard_map/border_and_down/pallas_call | solution.py:217
  27.1 4.9 %collective-permute-start.8 = (f32[128,1024]{1,0:T(8,128)S(1)}, f32[128,1024]{1,0:T(8,128)S(1)}, u32[]{:S(2)}, u32[]{:S(2)}) collective-permute-start(f32[128,1024]{1,0:T(8,128)S(1)} %get-tuple-element.25.below), channel_id=1, source_target_pairs={{0,2},{2,4},{4,6},{6,8},{8,10},{10,12},{12,14},{14,16},{16,18},{18... | collective-permute-start | bytes 1572872 | tf_op jit(solution)/shard_map/ppermute | solution.py:20
  32.0 0.0 collective-permute-done.5.rest_1_
  32.0 0.1 collective-permute-start.6
  32.1 1.2 %collective-permute-done.6.half = f32[16,512]{1,0:T(8,128)S(1)} collective-permute-done((f32[16,512]{1,0:T(8,128)S(1)}, f32[16,512]{1,0:T(8,128)S(1)}, u32[]{:S(2)}, u32[]{:S(2)}) %collective-permute-start.6) | collective-permute-done | bytes 32800 | tf_op jit(solution)/shard_map/ppermute | solution.py:25
  33.3 1.6 %second_border.1 = (f32[128,1024]{1,0:T(8,128)S(1)}, f32[128,768]{1,0:T(8,128)S(1)}, f32[128,256]{1,0:T(8,128)S(1)}) custom-call(s32[4]{0:T(128)S(1)} %copy-done.5, s32[4]{0:T(128)S(1)} %copy-done.6, f32[128,1024]{1,0:T(8,128)S(1)} %get-tuple-element.25.below, f32[256,1024]{1,0:T(8,128)S(1)} %get-tuple-element.26.cd, ...), custom_call_target="tpu_custom_call" | custom-call | flops 1 | bytes 1 | tf_op jit(solution)/shard_map/second_border/pallas_call | solution.py:217
  34.9 2.5 %collective-permute-start.9 = (f32[128,768]{1,0:T(8,128)S(1)}, f32[128,768]{1,0:T(8,128)S(1)}, u32[]{:S(2)}, u32[]{:S(2)}) collective-permute-start(f32[128,768]{1,0:T(8,128)S(1)} %get-tuple-element.34), channel_id=1, source_target_pairs={{0,2},{2,4},{4,6},{6,8},{8,10},{10,12},{12,14},{14,16},{16,18},{18... | collective-permute-start | bytes 1179656 | tf_op jit(solution)/shard_map/ppermute | solution.py:20
  37.4 5.2 %collective-permute-start.7 = (f32[128,256]{1,0:T(8,128)S(1)}, f32[128,256]{1,0:T(8,128)S(1)}, u32[]{:S(2)}, u32[]{:S(2)}) collective-permute-start(f32[128,256]{1,0:T(8,128)S(1)} %get-tuple-element.29), channel_id=1, source_target_pairs={{0,2},{2,4},{4,6},{6,8},{8,10},{10,12},{12,14},{14,16},{16,18},{18... | collective-permute-start | bytes 393224 | tf_op jit(solution)/shard_map/ppermute | solution.py:20
  42.6 1.7 %collective-permute-done.8.above = f32[128,1024]{1,0:T(8,128)S(1)} collective-permute-done((f32[128,1024]{1,0:T(8,128)S(1)}, f32[128,1024]{1,0:T(8,128)S(1)}, u32[]{:S(2)}, u32[]{:S(2)}) %collective-permute-start.8) | collective-permute-done | bytes 524320 | tf_op jit(solution)/shard_map/ppermute | solution.py:20
  44.3 3.7 %rest.1 = (f32[512,1024]{1,0:T(8,128)}, f32[256,768]{1,0:T(8,128)S(1)}, f32[256,256]{1,0:T(8,128)S(1)}) custom-call(s32[4]{0:T(128)S(1)} %copy-done.5, s32[4]{0:T(128)S(1)} %copy-done.6, f32[512,1024]{1,0:T(8,128)S(1)} %copy-done, f32[128,1024]{1,0:T(8,128)S(1)} %collective-permute-done.8.above, f32[256,1024]{1,0:T(8,128)S(1)} %get-tuple-element.23.c.bc, ...), custom_call_target="tpu_custom_call" | custom-call | flops 1 | bytes 1 | tf_op jit(solution)/shard_map/rest/pallas_call | solution.py:217
  48.1 4.0 %collective-permute-done.9.above = f32[128,768]{1,0:T(8,128)S(1)} collective-permute-done((f32[128,768]{1,0:T(8,128)S(1)}, f32[128,768]{1,0:T(8,128)S(1)}, u32[]{:S(2)}, u32[]{:S(2)}) %collective-permute-start.9) | collective-permute-done | bytes 393248 | tf_op jit(solution)/shard_map/ppermute | solution.py:20
  52.1 1.4 %finish.2.out_in = f32[512,1024]{1,0:T(8,128)} custom-call(f32[128,768]{1,0:T(8,128)S(1)} %collective-permute-done.9.above, f32[2,256,256]{2,1,0:T(8,128)S(1)} %get-tuple-element.30.late, f32[256,768]{1,0:T(8,128)S(1)} %get-tuple-element.35.before, f32[512,1024]{1,0:T(8,128)} %get-tuple-element.36.out_in), custom_call_target="tpu_custom_call", output_to_operand_aliasing={{}: (3, {})} | custom-call | flops 1 | bytes 1 | tf_op jit(solution)/shard_map/finish/pallas_call | solution.py:217
  53.4 0.0 collective-permute-done.7.above
  53.5 1.0 %finish.3 = f32[512,1024]{1,0:T(8,128)} custom-call(f32[128,256]{1,0:T(8,128)S(1)} %collective-permute-done.7.above, f32[2,256,256]{2,1,0:T(8,128)S(1)} %get-tuple-element.30.late, f32[256,256]{1,0:T(8,128)S(1)} %get-tuple-element.33.before, f32[512,1024]{1,0:T(8,128)} %finish.2.out_in), custom_call_target="tpu_custom_call", output_to_operand_aliasing={{}: (3, {})} | custom-call | flops 1 | bytes 1 | tf_op jit(solution)/shard_map/finish/pallas_call | solution.py:217
  (1 shorter events, 0.0 us)
Async XLA Ops:
  0.0 12.2 %copy-start.1 = (f32[1,4,128,128]{3,2,1,0:T(8,128)S(1)}, f32[1,4,128,128]{3,2,1,0:T(8,128)}, u32[]{:S(2)}) copy-start(f32[1,4,128,128]{3,2,1,0:T(8,128)} %param.8) | copy-start | bytes 786436
  0.0 12.2 %copy-start.3 = (f32[1,4,128,128]{3,2,1,0:T(8,128)S(1)}, f32[1,4,128,128]{3,2,1,0:T(8,128)}, u32[]{:S(2)}) copy-start(f32[1,4,128,128]{3,2,1,0:T(8,128)} %param.10) | copy-start | bytes 786436
  0.0 12.2 %copy-start.2 = (f32[1,4,128,128]{3,2,1,0:T(8,128)S(1)}, f32[1,4,128,128]{3,2,1,0:T(8,128)}, u32[]{:S(2)}) copy-start(f32[1,4,128,128]{3,2,1,0:T(8,128)} %param.9) | copy-start | bytes 786436
  0.0 12.2 %copy-start.4 = (f32[1,4,128,128]{3,2,1,0:T(8,128)S(1)}, f32[1,4,128,128]{3,2,1,0:T(8,128)}, u32[]{:S(2)}) copy-start(f32[1,4,128,128]{3,2,1,0:T(8,128)} %param.11) | copy-start | bytes 786436
  1.2 23.2 %collective-permute-start = (f32[128,1024]{1,0:T(8,128)S(1)}, f32[128,1024]{1,0:T(8,128)S(1)}, u32[]{:S(2)}, u32[]{:S(2)}) collective-permute-start(f32[128,1024]{1,0:T(8,128)S(1)} %slice.24), channel_id=1, source_target_pairs={{2,0},{4,2},{6,4},{8,6},{10,8},{12,10},{14,12},{16,14},{18,16},{20... | collective-permute-start | bytes 1572872 | tf_op jit(solution)/shard_map/ppermute | solution.py:20
  3.5 1.7 %collective-permute-start.1 = (f32[2,128,128]{2,1,0:T(8,128)S(1)}, f32[2,128,128]{2,1,0:T(8,128)S(1)}, u32[]{:S(2)}, u32[]{:S(2)}) collective-permute-start(f32[2,128,128]{2,1,0:T(8,128)S(1)} %get-tuple-element.38.own), channel_id=1, source_target_pairs={{0,1},{1,0},{2,3},{3,2},{4,5},{5,4},{6,7},{7,6},{8,9},{9,8},{10,11... | collective-permute-start | bytes 393224 | tf_op jit(solution)/shard_map/ppermute | solution.py:25
  4.0 20.4 %copy-start = (f32[512,1024]{1,0:T(8,128)S(1)}, f32[512,1024]{1,0:T(8,128)}, u32[]{:S(2)}) copy-start(f32[512,1024]{1,0:T(8,128)} %raw.1) | copy-start | bytes 6291460
  4.0 20.4 %copy-start.5 = (s32[4]{0:T(128)S(1)}, s32[4]{0:T(128)}, u32[]{:S(2)}) copy-start(s32[4]{0:T(128)} %starts.5) | copy-start | bytes 52
  4.0 20.4 %copy-start.6 = (s32[4]{0:T(128)S(1)}, s32[4]{0:T(128)}, u32[]{:S(2)}) copy-start(s32[4]{0:T(128)} %spans.5) | copy-start | bytes 52
  4.0 8.1 %collective-permute-start.4 = (f32[4,128,128]{2,1,0:T(8,128)}, f32[4,128,128]{2,1,0:T(8,128)S(1)}, u32[]{:S(2)}, u32[]{:S(2)}) collective-permute-start(f32[4,128,128]{2,1,0:T(8,128)} %bitcast.12), channel_id=1, source_target_pairs={{0,1},{1,0},{2,3},{3,2},{4,5},{5,4},{6,7},{7,6},{8,9},{9,8},{10,11... | collective-permute-start | bytes 786440 | tf_op jit(solution)/shard_map/ppermute | solution.py:25
  8.0 16.4 %collective-permute-start.2 = (f32[128,512]{1,0:T(8,128)S(1)}, f32[128,512]{1,0:T(8,128)S(1)}, u32[]{:S(2)}, u32[]{:S(2)}) collective-permute-start(f32[128,512]{1,0:T(8,128)S(1)} %get-tuple-element.21), channel_id=1, source_target_pairs={{2,0},{4,2},{6,4},{8,6},{10,8},{12,10},{14,12},{16,14},{18,16},{20... | collective-permute-start | bytes 786440 | tf_op jit(solution)/shard_map/ppermute | solution.py:20
  9.3 22.7 %collective-permute-start.5 = (f32[144,512]{1,0:T(8,128)S(1)}, f32[144,512]{1,0:T(8,128)S(1)}, u32[]{:S(2)}, u32[]{:S(2)}) collective-permute-start(f32[144,512]{1,0:T(8,128)S(1)} %get-tuple-element.27), channel_id=1, source_target_pairs={{2,0},{4,2},{6,4},{8,6},{10,8},{12,10},{14,12},{16,14},{18,16},{20... | collective-permute-start | bytes 884744 | tf_op jit(solution)/shard_map/ppermute | solution.py:20
  10.6 1.5 %collective-permute-start.3 = (f32[2,128,128]{2,1,0:T(8,128)S(1)}, f32[2,128,128]{2,1,0:T(8,128)S(1)}, u32[]{:S(2)}, u32[]{:S(2)}) collective-permute-start(f32[2,128,128]{2,1,0:T(8,128)S(1)} %get-tuple-element.37), channel_id=1, source_target_pairs={{0,1},{1,0},{2,3},{3,2},{4,5},{5,4},{6,7},{7,6},{8,9},{9,8},{10,11... | collective-permute-start | bytes 393224 | tf_op jit(solution)/shard_map/ppermute | solution.py:25
  27.1 17.2 %collective-permute-start.8 = (f32[128,1024]{1,0:T(8,128)S(1)}, f32[128,1024]{1,0:T(8,128)S(1)}, u32[]{:S(2)}, u32[]{:S(2)}) collective-permute-start(f32[128,1024]{1,0:T(8,128)S(1)} %get-tuple-element.25.below), channel_id=1, source_target_pairs={{0,2},{2,4},{4,6},{6,8},{8,10},{10,12},{12,14},{14,16},{16,18},{18... | collective-permute-start | bytes 1572872 | tf_op jit(solution)/shard_map/ppermute | solution.py:20
  32.0 1.3 %collective-permute-start.6 = (f32[16,512]{1,0:T(8,128)S(1)}, f32[16,512]{1,0:T(8,128)S(1)}, u32[]{:S(2)}, u32[]{:S(2)}) collective-permute-start(f32[16,512]{1,0:T(8,128)S(1)} %slice.32), channel_id=1, source_target_pairs={{0,1},{1,0},{2,3},{3,2},{4,5},{5,4},{6,7},{7,6},{8,9},{9,8},{10,11... | collective-permute-start | bytes 98312 | tf_op jit(solution)/shard_map/ppermute | solution.py:25
  34.9 17.1 %collective-permute-start.9 = (f32[128,768]{1,0:T(8,128)S(1)}, f32[128,768]{1,0:T(8,128)S(1)}, u32[]{:S(2)}, u32[]{:S(2)}) collective-permute-start(f32[128,768]{1,0:T(8,128)S(1)} %get-tuple-element.34), channel_id=1, source_target_pairs={{0,2},{2,4},{4,6},{6,8},{8,10},{10,12},{12,14},{14,16},{16,18},{18... | collective-permute-start | bytes 1179656 | tf_op jit(solution)/shard_map/ppermute | solution.py:20
  37.4 16.0 %collective-permute-start.7 = (f32[128,256]{1,0:T(8,128)S(1)}, f32[128,256]{1,0:T(8,128)S(1)}, u32[]{:S(2)}, u32[]{:S(2)}) collective-permute-start(f32[128,256]{1,0:T(8,128)S(1)} %get-tuple-element.29), channel_id=1, source_target_pairs={{0,2},{2,4},{4,6},{6,8},{8,10},{10,12},{12,14},{14,16},{16,18},{18... | collective-permute-start | bytes 393224 | tf_op jit(solution)/shard_map/ppermute | solution.py:20

commit v5 on v4

--- a/solution.py
+++ b/solution.py
@@ -9,6 +9,7 @@
 
 F32 = jnp.float32
 TILES = 2
+CHUNK = 256
 EIGHTHS_UP = (4, 4)
 EIGHTHS_DOWN = (6, 2)
 VMEM_LIMIT = 24 * 1024 * 1024
@@ -31,17 +32,14 @@
 
 
 def dot(x, y, contract=(1, 0)):
-    def product(left, right):
-        return lax.dot_general(
-            left,
-            right,
-            (((contract[0],), (contract[1],)), ((), ())),
-            preferred_element_type=F32,
-        )
-
     xh, xl = split(x)
     yh, yl = split(y)
-    return product(xl, yh) + product(xh, yl) + product(xh, yh)
+    return lax.dot_general(
+        jnp.concatenate([xl, xh, xh], axis=contract[0]),
+        jnp.concatenate([yh, yl, yh], axis=contract[1]),
+        (((contract[0],), (contract[1],)), ((), ())),
+        preferred_element_type=F32,
+    )
 
 
 def exact_dot(x, y):
@@ -183,16 +181,30 @@
         copy.wait()
 
 
-def last_kernel(cut, above, late, before, out_in, out, held, sem):
+def last_kernel(cut, above, late, before, out_in, out, held, sems):
     del out_in
-    width = above.shape[0]
-    top = above[...]
-    change = dot(late[0], top)
-    held[:width] = before[:width] + (top - change[:width])
-    held[width:] = before[width:] - change[width:]
-    copy = pltpu.make_async_copy(held, out.at[pl.ds(0, 2 * width), cut], sem)
-    copy.start()
-    copy.wait()
+    width, span = above.shape
+    high, low = split(late[0])
+    matrix = jnp.concatenate([low, high, high], axis=1)
+    copies = []
+    for at in range(span // CHUNK):
+        here = slice(at * CHUNK, (at + 1) * CHUNK)
+        top = above[:, here]
+        high, low = split(top)
+        change = jnp.dot(
+            matrix, jnp.concatenate([high, low, high], axis=0), preferred_element_type=F32
+        )
+        held[:width, here] = before[:width, here] + (top - change[:width])
+        held[width:, here] = before[width:, here] - change[width:]
+        copy = pltpu.make_async_copy(
+            held.at[:, here],
+            out.at[pl.ds(0, 2 * width), pl.ds(cut.start + at * CHUNK, CHUNK)],
+            sems.at[at],
+        )
+        copy.start()
+        copies.append(copy)
+    for copy in copies:
+        copy.wait()
 
 
 def smem():
@@ -314,7 +326,10 @@
             [(height, cols)],
             [part, late, kept, out],
             "finish",
-            scratch_shapes=[pltpu.VMEM((2 * width, down), F32), pltpu.SemaphoreType.DMA],
+            scratch_shapes=[
+                pltpu.VMEM((2 * width, down), F32),
+                pltpu.SemaphoreType.DMA((down // CHUNK,)),
+            ],
             input_output_aliases={3: 0},
         )
     return out

time: 54.8 us -> 54.7 us (level)
  Pallas kernels: 14.6 us -> 13.9 us
  waiting for transfers between devices: 18.8 us -> 19.4 us
    pallas_call x7, Pallas kernels: 14.6 us -> 13.9 us  [call(): pl.pallas_call(kernel, grid=(tiles,), in_specs=in_specs, out_specs=out_sp...]
    ppermute x6, waiting for transfers between devices: 16.6 us -> 17.2 us  [from_behind(): return lax.ppermute(value, axis, pairs)]
  transfers between devices with their start and end apart: 10 -> 10, of which waited for: 5 -> 6; matrix products, arithmetic and copies ran while one was open for 4% -> 4% of each run, Pallas kernels for 25% -> 24%
where the time goes in v5:
time: 54.7 us; the launch traced here: 54.4 us
  waiting for transfers between devices  19.4 us (35%)
  starting transfers between devices  17.7 us (32%)
  Pallas kernels  13.9 us (25%)
  local copies, waits for them, and re-layouts  3.23 us (6%)
    ppermute x6, waiting for transfers between devices, from_behind(): return lax.ppermute(value, axis, pairs)  17.2 us
    ppermute x6, starting transfers between devices, from_behind(): return lax.ppermute(value, axis, pairs)  16.4 us
    pallas_call x7, Pallas kernels, call(): pl.pallas_call(kernel, grid=(tiles,), in_specs=in_specs, out_specs=out_sp...  13.9 us
    ppermute x4, waiting for transfers between devices, other_core(): lax.ppermute(value, 'col', [(i, (i + 1) % cores) for i in range(cores)])  2.19 us
    ppermute x4, starting transfers between devices, other_core(): lax.ppermute(value, 'col', [(i, (i + 1) % cores) for i in range(cores)])  1.24 us
    slice x1, local copies, waits for them, and re-layouts, local(): below = from_behind(panel[:width], 'row', -1)  1.17 us
  transfers between devices with their start and end apart: 10, of which 6 were waited for; matrix products, arithmetic and copies ran while one was open for 4% of the time, Pallas kernels for 24%

profile of v5, /device:TPU:0, one launch (start us, length us, event | category | flops | bytes accessed | tf_op | source)
XLA Modules:
  0.0 54.4 jit_solution(5018753452907011682)
XLA Ops:
  0.0 0.0 copy-start.1
  0.0 0.0 copy-start.3
  0.0 0.0 copy-start.2
  0.0 0.0 copy-start.4
  0.0 1.2 %slice.24 = f32[128,1024]{1,0:T(8,128)S(1)} slice(f32[512,1024]{1,0:T(8,128)} %raw.1), slice={[0:128], [0:1024]} | slice | bytes 1048576 | tf_op jit(solution)/shard_map/slice | solution.py:250
  1.2 1.3 %collective-permute-start = (f32[128,1024]{1,0:T(8,128)S(1)}, f32[128,1024]{1,0:T(8,128)S(1)}, u32[]{:S(2)}, u32[]{:S(2)}) collective-permute-start(f32[128,1024]{1,0:T(8,128)S(1)} %slice.24), channel_id=1, source_target_pairs={{2,0},{4,2},{6,4},{8,6},{10,8},{12,10},{14,12},{16,14},{18,16},{20... | collective-permute-start | bytes 1572872 | tf_op jit(solution)/shard_map/ppermute | solution.py:21
  2.5 1.0 %slice_bitcast_fusion = (f32[2,128,128]{2,1,0:T(8,128)S(1)}, f32[2,128,128]{2,1,0:T(8,128)S(1)}) fusion(f32[1,4,128,128]{3,2,1,0:T(8,128)} %param.8), kind=kLoop, calls=%fused_computation | loop fusion | bytes 524288 | tf_op jit(solution)/shard_map/slice | solution.py:253
  3.5 0.5 collective-permute-start.1
  4.0 0.0 copy-start
  4.0 0.0 copy-start.5
  4.0 0.0 copy-start.6
  4.0 0.1 collective-permute-start.4
  4.1 1.0 %slice_bitcast_fusion.1.factor = f32[2,128,128]{2,1,0:T(8,128)S(1)} fusion(f32[1,4,128,128]{3,2,1,0:T(8,128)} %param.9), kind=kLoop, calls=%fused_computation.1 | loop fusion | bytes 262144 | tf_op jit(solution)/shard_map/slice | solution.py:251
  5.2 0.0 collective-permute-done.1.other
  5.2 2.6 %inner_and_up.1 = (f32[2,256,256]{2,1,0:T(8,128)S(1)}, f32[256,1024]{1,0:T(8,128)S(1)}, f32[128,512]{1,0:T(8,128)S(1)}, f32[144,512]{1,0:T(8,128)S(1)}) custom-call(f32[2,128,128]{2,1,0:T(8,128)S(1)} %get-tuple-element.38.own, f32[2,128,128]{2,1,0:T(8,128)S(1)} %collective-permute-done.1.other, f32[2,128,128]{2,1,0:T(8,128)S(1)} %slice_bitcast_fusion.1.factor, ...), custom_call_target="tpu_custom_call" | custom-call | flops 1 | bytes 1 | tf_op jit(solution)/shard_map/inner_and_up/pallas_call | solution.py:229
  7.8 1.3 %collective-permute-start.2 = (f32[128,512]{1,0:T(8,128)S(1)}, f32[128,512]{1,0:T(8,128)S(1)}, u32[]{:S(2)}, u32[]{:S(2)}) collective-permute-start(f32[128,512]{1,0:T(8,128)S(1)} %get-tuple-element.21), channel_id=1, source_target_pairs={{2,0},{4,2},{6,4},{8,6},{10,8},{12,10},{14,12},{16,14},{18,16},{20... | collective-permute-start | bytes 786440 | tf_op jit(solution)/shard_map/ppermute | solution.py:21
  9.1 1.3 %collective-permute-start.5 = (f32[144,512]{1,0:T(8,128)S(1)}, f32[144,512]{1,0:T(8,128)S(1)}, u32[]{:S(2)}, u32[]{:S(2)}) collective-permute-start(f32[144,512]{1,0:T(8,128)S(1)} %get-tuple-element.27), channel_id=1, source_target_pairs={{2,0},{4,2},{6,4},{8,6},{10,8},{12,10},{14,12},{16,14},{18,16},{20... | collective-permute-start | bytes 884744 | tf_op jit(solution)/shard_map/ppermute | solution.py:21
  10.4 0.5 collective-permute-start.3
  10.9 1.0 %collective-permute-done.3.other_i = f32[2,128,128]{2,1,0:T(8,128)S(1)} collective-permute-done((f32[2,128,128]{2,1,0:T(8,128)S(1)}, f32[2,128,128]{2,1,0:T(8,128)S(1)}, u32[]{:S(2)}, u32[]{:S(2)}) %collective-permute-start.3) | collective-permute-done | bytes 131104 | tf_op jit(solution)/shard_map/ppermute | solution.py:26
  11.9 0.0 collective-permute-done.4.other_b
  11.9 0.0 copy-done.1
  11.9 0.0 copy-done.3
  11.9 0.0 copy-done.2
  11.9 0.0 copy-done.4
  11.9 1.2 %matrices.1 = (f32[2,256,256]{2,1,0:T(8,128)S(1)}, f32[4,256,256]{2,1,0:T(8,128)S(1)}) custom-call(f32[4,128,128]{2,1,0:T(8,128)S(1)} %bitcast.10, f32[2,128,128]{2,1,0:T(8,128)S(1)} %collective-permute-done.3.other_i, f32[4,128,128]{2,1,0:T(8,128)S(1)} %bitcast.11, f32[4,128,128]{2,1,0:T(8,128)S(1)} %bitcast.13, ...), custom_call_target="tpu_custom_call" | custom-call | flops 1 | bytes 1 | tf_op jit(solution)/shard_map/matrices/pallas_call | solution.py:229
  13.2 11.2 %collective-permute-done.2.rest_0_ = f32[128,512]{1,0:T(8,128)S(1)} collective-permute-done((f32[128,512]{1,0:T(8,128)S(1)}, f32[128,512]{1,0:T(8,128)S(1)}, u32[]{:S(2)}, u32[]{:S(2)}) %collective-permute-start.2) | collective-permute-done | bytes 262176 | tf_op jit(solution)/shard_map/ppermute | solution.py:21
  24.4 0.0 collective-permute-done.below
  24.4 0.0 copy-done
  24.4 0.0 copy-done.5
  24.4 0.0 copy-done.6
  24.4 2.7 %border_and_down.1 = (f32[128,1024]{1,0:T(8,128)S(1)}, f32[256,1024]{1,0:T(8,128)S(1)}) custom-call(s32[4]{0:T(128)S(1)} %copy-done.5, s32[4]{0:T(128)S(1)} %copy-done.6, f32[512,1024]{1,0:T(8,128)S(1)} %copy-done, f32[128,1024]{1,0:T(8,128)S(1)} %collective-permute-done.below, f32[256,1024]{1,0:T(8,128)S(1)} %get-tuple-element.23.c.bc, ...), custom_call_target="tpu_custom_call" | custom-call | flops 1 | bytes 1 | tf_op jit(solution)/shard_map/border_and_down/pallas_call | solution.py:229
  27.1 4.9 %collective-permute-start.8 = (f32[128,1024]{1,0:T(8,128)S(1)}, f32[128,1024]{1,0:T(8,128)S(1)}, u32[]{:S(2)}, u32[]{:S(2)}) collective-permute-start(f32[128,1024]{1,0:T(8,128)S(1)} %get-tuple-element.25.below), channel_id=1, source_target_pairs={{0,2},{2,4},{4,6},{6,8},{8,10},{10,12},{12,14},{14,16},{16,18},{18... | collective-permute-start | bytes 1572872 | tf_op jit(solution)/shard_map/ppermute | solution.py:21
  32.0 0.0 collective-permute-done.5.rest_1_
  32.0 0.1 collective-permute-start.6
  32.1 1.2 %collective-permute-done.6.half = f32[16,512]{1,0:T(8,128)S(1)} collective-permute-done((f32[16,512]{1,0:T(8,128)S(1)}, f32[16,512]{1,0:T(8,128)S(1)}, u32[]{:S(2)}, u32[]{:S(2)}) %collective-permute-start.6) | collective-permute-done | bytes 32800 | tf_op jit(solution)/shard_map/ppermute | solution.py:26
  33.3 1.6 %second_border.1 = (f32[128,1024]{1,0:T(8,128)S(1)}, f32[128,768]{1,0:T(8,128)S(1)}, f32[128,256]{1,0:T(8,128)S(1)}) custom-call(s32[4]{0:T(128)S(1)} %copy-done.5, s32[4]{0:T(128)S(1)} %copy-done.6, f32[128,1024]{1,0:T(8,128)S(1)} %get-tuple-element.25.below, f32[256,1024]{1,0:T(8,128)S(1)} %get-tuple-element.26.cd, ...), custom_call_target="tpu_custom_call" | custom-call | flops 1 | bytes 1 | tf_op jit(solution)/shard_map/second_border/pallas_call | solution.py:229
  34.9 2.5 %collective-permute-start.9 = (f32[128,768]{1,0:T(8,128)S(1)}, f32[128,768]{1,0:T(8,128)S(1)}, u32[]{:S(2)}, u32[]{:S(2)}) collective-permute-start(f32[128,768]{1,0:T(8,128)S(1)} %get-tuple-element.34), channel_id=1, source_target_pairs={{0,2},{2,4},{4,6},{6,8},{8,10},{10,12},{12,14},{14,16},{16,18},{18... | collective-permute-start | bytes 1179656 | tf_op jit(solution)/shard_map/ppermute | solution.py:21
  37.4 5.2 %collective-permute-start.7 = (f32[128,256]{1,0:T(8,128)S(1)}, f32[128,256]{1,0:T(8,128)S(1)}, u32[]{:S(2)}, u32[]{:S(2)}) collective-permute-start(f32[128,256]{1,0:T(8,128)S(1)} %get-tuple-element.29), channel_id=1, source_target_pairs={{0,2},{2,4},{4,6},{6,8},{8,10},{10,12},{12,14},{14,16},{16,18},{18... | collective-permute-start | bytes 393224 | tf_op jit(solution)/shard_map/ppermute | solution.py:21
  42.5 1.8 %collective-permute-done.8.above = f32[128,1024]{1,0:T(8,128)S(1)} collective-permute-done((f32[128,1024]{1,0:T(8,128)S(1)}, f32[128,1024]{1,0:T(8,128)S(1)}, u32[]{:S(2)}, u32[]{:S(2)}) %collective-permute-start.8) | collective-permute-done | bytes 524320 | tf_op jit(solution)/shard_map/ppermute | solution.py:21
  44.3 3.7 %rest.1 = (f32[512,1024]{1,0:T(8,128)}, f32[256,768]{1,0:T(8,128)S(1)}, f32[256,256]{1,0:T(8,128)S(1)}) custom-call(s32[4]{0:T(128)S(1)} %copy-done.5, s32[4]{0:T(128)S(1)} %copy-done.6, f32[512,1024]{1,0:T(8,128)S(1)} %copy-done, f32[128,1024]{1,0:T(8,128)S(1)} %collective-permute-done.8.above, f32[256,1024]{1,0:T(8,128)S(1)} %get-tuple-element.23.c.bc, ...), custom_call_target="tpu_custom_call" | custom-call | flops 1 | bytes 1 | tf_op jit(solution)/shard_map/rest/pallas_call | solution.py:229
  48.1 4.0 %collective-permute-done.9.above = f32[128,768]{1,0:T(8,128)S(1)} collective-permute-done((f32[128,768]{1,0:T(8,128)S(1)}, f32[128,768]{1,0:T(8,128)S(1)}, u32[]{:S(2)}, u32[]{:S(2)}) %collective-permute-start.9) | collective-permute-done | bytes 393248 | tf_op jit(solution)/shard_map/ppermute | solution.py:21
  52.1 1.2 %finish.2.out_in = f32[512,1024]{1,0:T(8,128)} custom-call(f32[128,768]{1,0:T(8,128)S(1)} %collective-permute-done.9.above, f32[2,256,256]{2,1,0:T(8,128)S(1)} %get-tuple-element.30.late, f32[256,768]{1,0:T(8,128)S(1)} %get-tuple-element.35.before, f32[512,1024]{1,0:T(8,128)} %get-tuple-element.36.out_in), custom_call_target="tpu_custom_call", output_to_operand_aliasing={{}: (3, {})} | custom-call | flops 1 | bytes 1 | tf_op jit(solution)/shard_map/finish/pallas_call | solution.py:229
  53.3 0.2 collective-permute-done.7.above
  53.5 0.9 %finish.3 = f32[512,1024]{1,0:T(8,128)} custom-call(f32[128,256]{1,0:T(8,128)S(1)} %collective-permute-done.7.above, f32[2,256,256]{2,1,0:T(8,128)S(1)} %get-tuple-element.30.late, f32[256,256]{1,0:T(8,128)S(1)} %get-tuple-element.33.before, f32[512,1024]{1,0:T(8,128)} %finish.2.out_in), custom_call_target="tpu_custom_call", output_to_operand_aliasing={{}: (3, {})} | custom-call | flops 1 | bytes 1 | tf_op jit(solution)/shard_map/finish/pallas_call | solution.py:229
  (1 shorter events, 0.0 us)
Async XLA Ops:
  0.0 11.9 %copy-start.1 = (f32[1,4,128,128]{3,2,1,0:T(8,128)S(1)}, f32[1,4,128,128]{3,2,1,0:T(8,128)}, u32[]{:S(2)}) copy-start(f32[1,4,128,128]{3,2,1,0:T(8,128)} %param.8) | copy-start | bytes 786436
  0.0 11.9 %copy-start.3 = (f32[1,4,128,128]{3,2,1,0:T(8,128)S(1)}, f32[1,4,128,128]{3,2,1,0:T(8,128)}, u32[]{:S(2)}) copy-start(f32[1,4,128,128]{3,2,1,0:T(8,128)} %param.10) | copy-start | bytes 786436
  0.0 11.9 %copy-start.2 = (f32[1,4,128,128]{3,2,1,0:T(8,128)S(1)}, f32[1,4,128,128]{3,2,1,0:T(8,128)}, u32[]{:S(2)}) copy-start(f32[1,4,128,128]{3,2,1,0:T(8,128)} %param.9) | copy-start | bytes 786436
  0.0 11.9 %copy-start.4 = (f32[1,4,128,128]{3,2,1,0:T(8,128)S(1)}, f32[1,4,128,128]{3,2,1,0:T(8,128)}, u32[]{:S(2)}) copy-start(f32[1,4,128,128]{3,2,1,0:T(8,128)} %param.11) | copy-start | bytes 786436
  1.2 23.2 %collective-permute-start = (f32[128,1024]{1,0:T(8,128)S(1)}, f32[128,1024]{1,0:T(8,128)S(1)}, u32[]{:S(2)}, u32[]{:S(2)}) collective-permute-start(f32[128,1024]{1,0:T(8,128)S(1)} %slice.24), channel_id=1, source_target_pairs={{2,0},{4,2},{6,4},{8,6},{10,8},{12,10},{14,12},{16,14},{18,16},{20... | collective-permute-start | bytes 1572872 | tf_op jit(solution)/shard_map/ppermute | solution.py:21
  3.5 1.7 %collective-permute-start.1 = (f32[2,128,128]{2,1,0:T(8,128)S(1)}, f32[2,128,128]{2,1,0:T(8,128)S(1)}, u32[]{:S(2)}, u32[]{:S(2)}) collective-permute-start(f32[2,128,128]{2,1,0:T(8,128)S(1)} %get-tuple-element.38.own), channel_id=1, source_target_pairs={{0,1},{1,0},{2,3},{3,2},{4,5},{5,4},{6,7},{7,6},{8,9},{9,8},{10,11... | collective-permute-start | bytes 393224 | tf_op jit(solution)/shard_map/ppermute | solution.py:26
  4.0 20.4 %copy-start = (f32[512,1024]{1,0:T(8,128)S(1)}, f32[512,1024]{1,0:T(8,128)}, u32[]{:S(2)}) copy-start(f32[512,1024]{1,0:T(8,128)} %raw.1) | copy-start | bytes 6291460
  4.0 20.4 %copy-start.5 = (s32[4]{0:T(128)S(1)}, s32[4]{0:T(128)}, u32[]{:S(2)}) copy-start(s32[4]{0:T(128)} %starts.5) | copy-start | bytes 52
  4.0 20.4 %copy-start.6 = (s32[4]{0:T(128)S(1)}, s32[4]{0:T(128)}, u32[]{:S(2)}) copy-start(s32[4]{0:T(128)} %spans.5) | copy-start | bytes 52
  4.0 7.9 %collective-permute-start.4 = (f32[4,128,128]{2,1,0:T(8,128)}, f32[4,128,128]{2,1,0:T(8,128)S(1)}, u32[]{:S(2)}, u32[]{:S(2)}) collective-permute-start(f32[4,128,128]{2,1,0:T(8,128)} %bitcast.12), channel_id=1, source_target_pairs={{0,1},{1,0},{2,3},{3,2},{4,5},{5,4},{6,7},{7,6},{8,9},{9,8},{10,11... | collective-permute-start | bytes 786440 | tf_op jit(solution)/shard_map/ppermute | solution.py:26
  7.8 16.6 %collective-permute-start.2 = (f32[128,512]{1,0:T(8,128)S(1)}, f32[128,512]{1,0:T(8,128)S(1)}, u32[]{:S(2)}, u32[]{:S(2)}) collective-permute-start(f32[128,512]{1,0:T(8,128)S(1)} %get-tuple-element.21), channel_id=1, source_target_pairs={{2,0},{4,2},{6,4},{8,6},{10,8},{12,10},{14,12},{16,14},{18,16},{20... | collective-permute-start | bytes 786440 | tf_op jit(solution)/shard_map/ppermute | solution.py:21
  9.1 22.9 %collective-permute-start.5 = (f32[144,512]{1,0:T(8,128)S(1)}, f32[144,512]{1,0:T(8,128)S(1)}, u32[]{:S(2)}, u32[]{:S(2)}) collective-permute-start(f32[144,512]{1,0:T(8,128)S(1)} %get-tuple-element.27), channel_id=1, source_target_pairs={{2,0},{4,2},{6,4},{8,6},{10,8},{12,10},{14,12},{16,14},{18,16},{20... | collective-permute-start | bytes 884744 | tf_op jit(solution)/shard_map/ppermute | solution.py:21
  10.4 1.5 %collective-permute-start.3 = (f32[2,128,128]{2,1,0:T(8,128)S(1)}, f32[2,128,128]{2,1,0:T(8,128)S(1)}, u32[]{:S(2)}, u32[]{:S(2)}) collective-permute-start(f32[2,128,128]{2,1,0:T(8,128)S(1)} %get-tuple-element.37), channel_id=1, source_target_pairs={{0,1},{1,0},{2,3},{3,2},{4,5},{5,4},{6,7},{7,6},{8,9},{9,8},{10,11... | collective-permute-start | bytes 393224 | tf_op jit(solution)/shard_map/ppermute | solution.py:26
  27.1 17.2 %collective-permute-start.8 = (f32[128,1024]{1,0:T(8,128)S(1)}, f32[128,1024]{1,0:T(8,128)S(1)}, u32[]{:S(2)}, u32[]{:S(2)}) collective-permute-start(f32[128,1024]{1,0:T(8,128)S(1)} %get-tuple-element.25.below), channel_id=1, source_target_pairs={{0,2},{2,4},{4,6},{6,8},{8,10},{10,12},{12,14},{14,16},{16,18},{18... | collective-permute-start | bytes 1572872 | tf_op jit(solution)/shard_map/ppermute | solution.py:21
  32.0 1.3 %collective-permute-start.6 = (f32[16,512]{1,0:T(8,128)S(1)}, f32[16,512]{1,0:T(8,128)S(1)}, u32[]{:S(2)}, u32[]{:S(2)}) collective-permute-start(f32[16,512]{1,0:T(8,128)S(1)} %slice.32), channel_id=1, source_target_pairs={{0,1},{1,0},{2,3},{3,2},{4,5},{5,4},{6,7},{7,6},{8,9},{9,8},{10,11... | collective-permute-start | bytes 98312 | tf_op jit(solution)/shard_map/ppermute | solution.py:26
  34.9 17.2 %collective-permute-start.9 = (f32[128,768]{1,0:T(8,128)S(1)}, f32[128,768]{1,0:T(8,128)S(1)}, u32[]{:S(2)}, u32[]{:S(2)}) collective-permute-start(f32[128,768]{1,0:T(8,128)S(1)} %get-tuple-element.34), channel_id=1, source_target_pairs={{0,2},{2,4},{4,6},{6,8},{8,10},{10,12},{12,14},{14,16},{16,18},{18... | collective-permute-start | bytes 1179656 | tf_op jit(solution)/shard_map/ppermute | solution.py:21
  37.4 16.1 %collective-permute-start.7 = (f32[128,256]{1,0:T(8,128)S(1)}, f32[128,256]{1,0:T(8,128)S(1)}, u32[]{:S(2)}, u32[]{:S(2)}) collective-permute-start(f32[128,256]{1,0:T(8,128)S(1)} %get-tuple-element.29), channel_id=1, source_target_pairs={{0,2},{2,4},{4,6},{6,8},{8,10},{10,12},{12,14},{14,16},{16,18},{18... | collective-permute-start | bytes 393224 | tf_op jit(solution)/shard_map/ppermute | solution.py:21
